TPU v7x, 128 devices: a whole 4x4x4 slice. The times are simulated.
128 devices in a mesh: frame: 32 (over y, z, core), head: 4 (over x).
Axes of the slice: x: 4, y: 4, z: 4, core: 2. Of those that a mesh axis runs over, the one named last changes fastest.
Arguments:
- queries: bfloat16 [16384, 3072], P('frame', 'head'), may hold values from -240 to 240
- keys_in: bfloat16 [16384, 3072], P(('frame', 'head')), may hold values from -4 to 4
- values_in: bfloat16 [16384, 3072], P(('frame', 'head')), may hold values from -6 to 6
- grad_out: bfloat16 [16384, 3072], P('frame', 'head'), may hold values from -6 to 6
- assign: int32 [16384], P('frame'), may hold values from 0 to 127
- pattern: int32 [32, 16], replicated, may hold values from 0 to 63, as said below
- live_blocks: int32 [32], replicated, may hold values from 1 to 16, 256 in all
Outputs:
- attended: bfloat16 [16384, 3072], P('frame', 'head')
- grad_queries: bfloat16 [16384, 3072], P('frame', 'head')
- grad_keys: bfloat16 [16384, 3072], P(('frame', 'head'))
- grad_values: bfloat16 [16384, 3072], P(('frame', 'head'))
Inputs may be any that keep to these rules, and one draw needn't show every extreme that they name: `pattern`: each row names 16 different key blocks; row b begins with its own blocks b * 2 to (b + 1) * 2 - 1 in order; its other entries lie in frames other than b (block i lies in frame i // 2), at most 1 of them in any one frame, and exactly 1 in some frame of every row. `live_blocks`: at least 1, at most 16, and some query block attends all 16.
All inputs are finite; a program needn't handle non-finite values.
Results may differ from a plain program's by a relative error of at most 0.023.
The roundings to bfloat16 on the way count: a program that leaves them out, or rounds other values in their place, can miss the bound.
Values may be sent and summed in bfloat16 or wider, within the bound.
A program may use at most 128 MiB of HBM per device.

v0:
```python
import math

import jax
import jax.numpy as jnp
from jax import lax
from jax.experimental import pallas as pl
from jax.experimental.pallas import tpu as pltpu
from jax.sharding import PartitionSpec as P

HD = 128
KB = 64
NSEL = 16
SIDE = 4
CORES = 2
HEADS_X = 6
WIDTH = HEADS_X * HD
TOK = 512
TOK_DEV = TOK // SIDE
SLOTS = 128
UNITS = 6
CHUNK = 256
SCALE = 1.0 / math.sqrt(HD)
MESH = pl.DeviceIdType.MESH
BF = jnp.bfloat16
F32 = jnp.float32
VMEM_LIMIT = 56 * 1024 * 1024
STEPS = (1, -1, 2)
GROUPS = ((0, SIDE), (SIDE, HEADS_X - SIDE))
PARTS = ((0, 0), (1, 0), (0, 1), (1, 1))


class Place:
    def __init__(self):
        frame = lax.axis_index("frame")
        self.x = lax.axis_index("head")
        self.core = frame % CORES
        self.z = (frame // CORES) % SIDE
        self.y = frame // (CORES * SIDE)

    def device(self, y, z, core, x):
        return {"frame": (y * SIDE + z) * CORES + core, "head": x}

    def ring(self, axis, step):
        at = {"x": self.x, "y": self.y, "z": self.z}
        at[axis] = (at[axis] + step + SIDE) % SIDE
        return self.device(at["y"], at["z"], self.core, at["x"])

    def sibling(self):
        return self.device(self.y, self.z, 1 - self.core, self.x)

    def partner(self):
        return self.device(self.y, SIDE - 1 - self.z, self.core, self.x)


def shift(at, step):
    return (at + step + SIDE) % SIDE


def meet(place):
    partners = [place.sibling()]
    partners += [place.ring(axis, step) for axis in ("x", "z") for step in STEPS]
    partners += [place.ring("y", step) for step in (1, -1)]
    barrier = pltpu.get_barrier_semaphore()
    for target in partners:
        pl.semaphore_signal(barrier, inc=1, device_id=target, device_id_type=MESH)
    pl.semaphore_wait(barrier, len(partners))


class Links:
    def __init__(self, place, send, recv, local):
        self.send, self.recv, self.local = send, recv, local
        self.anyone = place.sibling()
        self.started = []
        self.names = {}
        self.local_names = {}

    def sem(self, name):
        return self.names.setdefault(name, len(self.names))

    def remote(self, name, src, dst, target):
        sem = self.sem(name)
        return pltpu.make_async_remote_copy(
            src_ref=src,
            dst_ref=dst,
            send_sem=self.send.at[sem],
            recv_sem=self.recv.at[sem],
            device_id=target,
            device_id_type=MESH,
        )

    def go(self, name, src, dst, target):
        copy = self.remote(name, src, dst, target)
        copy.start()
        self.started.append(copy)

    def got(self, name, region):
        self.remote(name, region, region, self.anyone).wait_recv()

    def here(self, name, src, dst):
        sem = self.local_names.setdefault(name, len(self.local_names))
        copy = pltpu.make_async_copy(src, dst, self.local.at[sem])
        copy.start()
        return copy

    def finish(self):
        for copy in self.started:
            copy.wait_send()


def low(ref):
    return ref.at[pl.ds(0, SIDE // 2)]


def high(ref):
    return ref.at[pl.ds(SIDE // 2, SIDE // 2)]


def cols(head, count=1):
    return pl.ds(pl.multiple_of(head * HD, HD), count * HD)


def token_rows(x):
    return pl.ds(pl.multiple_of(x * TOK_DEV, TOK_DEV), TOK_DEV)


def slot_hot_of(assign):
    slots = lax.broadcasted_iota(jnp.int32, (SLOTS, TOK), 0)
    return (slots == assign[0:1, :]).astype(F32)


def run_rounds(stages, stagger):
    ticks = {}
    for i, rounds in enumerate(stages):
        for r, step in enumerate(rounds):
            ticks.setdefault(i * stagger + r, []).append((-i, step))
    for tick in sorted(ticks):
        for _, step in sorted(ticks[tick], key=lambda item: item[0]):
            step()


GATHER_SEMS = len(PARTS) * 14 + 2 * 4
GATHER_LOCAL = len(PARTS) + 4


def gather_kernel(
    keys, values, queries, upstream, assign,
    every_key, every_value, query_out, upstream_out,
    tokens, merged, send, recv, local,
):
    place = Place()
    meet(place)
    links = Links(place, send, recv, local)
    sources = (keys, values)
    every = (every_key, every_value)
    own = {}

    def send_tokens(kv, slot):
        first, count = GROUPS[slot]
        for step in STEPS:
            links.go(
                ("x", kv, slot, step),
                sources[kv].at[:, cols(shift(place.x, step) * HEADS_X + first, count)],
                tokens.at[kv, token_rows(place.x), cols(first, count)],
                place.ring("x", step),
            )
        own[kv, slot] = links.here(
            ("x", kv, slot),
            sources[kv].at[:, cols(place.x * HEADS_X + first, count)],
            tokens.at[kv, token_rows(place.x), cols(first, count)],
        )

    def send_queries(which):
        src, dst = ((queries, query_out), (upstream, upstream_out))[which]
        for step in STEPS:
            links.go(
                ("q", which, step), src.at[:, cols(shift(place.z, step))], dst.at[place.z],
                place.ring("z", step),
            )
        mine = place.z // 2
        links.go(
            ("q", which, "partner"), src.at[:, cols(SIDE + 1 - mine)], dst.at[SIDE + 1],
            place.partner(),
        )
        own["q", which, 0] = links.here(("q", which, 0), src.at[:, cols(place.z)], dst.at[place.z])
        own["q", which, 1] = links.here(
            ("q", which, 1), src.at[:, cols(SIDE + mine)], dst.at[SIDE]
        )

    send_tokens(*PARTS[0])
    send_tokens(*PARTS[1])
    send_queries(0)
    send_tokens(*PARTS[2])
    send_tokens(*PARTS[3])
    hot = slot_hot_of(assign)
    divisor = jnp.maximum(jnp.sum(hot, axis=1, keepdims=True), 1.0)
    hot = hot.astype(BF)

    def stage(kv, slot):
        first, count = GROUPS[slot]
        out = every[kv]

        def region(step):
            return out.at[slot, shift(place.y, step), place.core]

        def pass_on(step):
            links.go(("s", kv, slot, step), region(step), region(step), place.sibling())

        def merge():
            own[kv, slot].wait()
            for step in STEPS:
                links.got(
                    ("x", kv, slot, step),
                    tokens.at[kv, token_rows(shift(place.x, -step)), cols(first, count)],
                )
            sums = jnp.dot(
                hot, tokens[kv, :, first * HD : (first + count) * HD], preferred_element_type=F32
            )
            mean = (sums / divisor).astype(BF)
            for i in range(count):
                merged[kv, first + i] = mean[:, i * HD : (i + 1) * HD]

            def head_of(z):
                return z if slot == 0 else SIDE + z // 2

            for step in STEPS:
                links.go(
                    ("z", kv, slot, step),
                    merged.at[kv, head_of(shift(place.z, step))],
                    out.at[slot, place.y, place.core, place.z],
                    place.ring("z", step),
                )
            out[slot, place.y, place.core, place.z] = merged[kv, head_of(place.z)]
            if (kv, slot) == PARTS[0]:
                send_queries(1)

        def row():
            for step in STEPS:
                links.got(
                    ("z", kv, slot, step),
                    out.at[slot, place.y, place.core, shift(place.z, -step)],
                )
            links.go(("y", kv, slot, 1), region(0), region(0), place.ring("y", 1))
            links.go(("y", kv, slot, -1), region(0), region(0), place.ring("y", -1))
            pass_on(0)

        def near():
            links.got(("y", kv, slot, 1), region(-1))
            links.go(("f", kv, slot, 1), low(region(-1)), low(region(-1)), place.ring("y", 1))
            pass_on(-1)
            links.got(("y", kv, slot, -1), region(1))
            links.go(("f", kv, slot, -1), high(region(1)), high(region(1)), place.ring("y", -1))
            pass_on(1)

        def far():
            links.got(("f", kv, slot, 1), low(region(2)))
            links.got(("f", kv, slot, -1), high(region(2)))
            pass_on(2)

        def close():
            for step in (0, -1, 1, 2):
                links.got(
                    ("s", kv, slot, step), out.at[slot, shift(place.y, step), 1 - place.core]
                )

        return [merge, row, near, far, close]

    run_rounds([stage(kv, slot) for kv, slot in PARTS], 1)
    for which, dst in enumerate((query_out, upstream_out)):
        for step in STEPS:
            links.got(("q", which, step), dst.at[shift(place.z, -step)])
        links.got(("q", which, "partner"), dst.at[SIDE + 1])
        own["q", which, 0].wait()
        own["q", which, 1].wait()
    links.finish()


def attention_kernel(
    pattern, live, keys, values, query, upstream,
    attended, query_grad, key_grad, value_grad,
    ksel, vsel, expo, kpart, vpart,
):
    place = Place()
    unit = pl.program_id(0)
    unit_z = jnp.where(unit < SIDE, unit, jnp.where(unit == SIDE, place.z, SIDE - 1 - place.z))
    frame = (place.y * SIDE + unit_z) * CORES + place.core
    count = live[frame]
    chunks = (count * KB + CHUNK - 1) // CHUNK
    rows_live = count * KB

    def spot_of(block):
        owner = block // 2
        y, z, core = owner // (CORES * SIDE), (owner // CORES) % SIDE, owner % CORES
        return ((y * CORES + core) * SIDE + z) * 2 + block % 2

    @pl.when((unit == 0) | (unit == SIDE))
    def _():
        key_grad[...] = jnp.zeros_like(key_grad)
        value_grad[...] = jnp.zeros_like(value_grad)

    for j in range(NSEL):
        spot = spot_of(pattern[frame, j])
        ksel[pl.ds(j * KB, KB), :] = keys[0, spot]
        vsel[pl.ds(j * KB, KB), :] = values[0, spot]
    q = query[0]
    g = upstream[0]
    q_t = q.T
    g_t = g.T

    def rows_of(c):
        return pl.ds(pl.multiple_of(c * CHUNK, CHUNK), CHUNK)

    def score_step(c, top):
        scores = jnp.dot(ksel[rows_of(c), :], q_t, preferred_element_type=F32) * SCALE
        ids = lax.broadcasted_iota(jnp.int32, (CHUNK, TOK), 0) + c * CHUNK
        scores = jnp.where(ids < rows_live, scores, -jnp.inf)
        expo[rows_of(c), :] = scores
        return jnp.maximum(top, jnp.max(scores, axis=0, keepdims=True))

    top = lax.fori_loop(0, chunks, score_step, jnp.full((1, TOK), -jnp.inf, F32))

    def value_step(c, state):
        total, weighted = state
        weights = jnp.exp(expo[rows_of(c), :] - top)
        expo[rows_of(c), :] = weights
        total = total + jnp.sum(weights, axis=0, keepdims=True)
        weighted = weighted + lax.dot_general(
            vsel[rows_of(c), :], weights.astype(BF), (((0,), (0,)), ((), ())),
            preferred_element_type=F32,
        )
        return total, weighted

    total, weighted = lax.fori_loop(
        0, chunks, value_step, (jnp.zeros((1, TOK), F32), jnp.zeros((HD, TOK), F32))
    )
    att_t = (weighted / total).astype(BF)
    attended[0] = att_t.T
    delta = jnp.sum(g_t.astype(F32) * att_t.astype(F32), axis=0, keepdims=True)
    inverse = 1.0 / total

    def grad_step(c, dq):
        probs = expo[rows_of(c), :] * inverse
        prob_grad = jnp.dot(vsel[rows_of(c), :], g_t, preferred_element_type=F32)
        score_grad = (probs * (prob_grad - delta)).astype(BF)
        kpart[rows_of(c), :] = jnp.dot(score_grad, q, preferred_element_type=F32) * SCALE
        vpart[rows_of(c), :] = jnp.dot(probs.astype(BF), g, preferred_element_type=F32)
        return dq + lax.dot_general(
            ksel[rows_of(c), :], score_grad, (((0,), (0,)), ((), ())), preferred_element_type=F32
        )

    dq = lax.fori_loop(0, chunks, grad_step, jnp.zeros((HD, TOK), F32))
    query_grad[0] = (dq * SCALE).astype(BF).T

    for j in range(NSEL):

        @pl.when(j < count)
        def _():
            spot = spot_of(pattern[frame, j])
            for out, part in ((key_grad, kpart), (value_grad, vpart)):
                piece = part[pl.ds(j * KB, KB), :].astype(BF).astype(F32)
                out[0, spot] = (out[0, spot].astype(F32) + piece).astype(BF)


SCATTER_SEMS = len(PARTS) * 14 + 2 * 4
SCATTER_LOCAL = len(PARTS) + 4


def scatter_kernel(
    key_part, value_part, att_in, dq_in, assign,
    attended, query_grad, grad_keys, grad_values,
    twin, halves, fulls, outgoing, column, pieces, tokens, send, recv, local,
):
    place = Place()
    meet(place)
    links = Links(place, send, recv, local)
    parts = (key_part, value_part)
    outs = (grad_keys, grad_values)
    own = []

    def send_twin(kv, slot):
        for step in (2, 1, -1, 0):
            y = shift(place.y, step)
            links.go(
                ("s", kv, slot, step), parts[kv].at[slot, y, 1 - place.core],
                twin.at[kv, slot, y], place.sibling(),
            )

    for kv, slot in PARTS:
        send_twin(kv, slot)
    mine = place.z // 2
    for which, (src, dst) in enumerate(((att_in, attended), (dq_in, query_grad))):
        for step in STEPS:
            links.go(
                ("q", which, step), src.at[shift(place.z, step)], dst.at[:, cols(place.z)],
                place.ring("z", step),
            )
        links.go(
            ("q", which, "partner"), src.at[SIDE + 1], dst.at[:, cols(SIDE + mine)],
            place.partner(),
        )
        own.append(links.here(("q", which, 0), src.at[place.z], dst.at[:, cols(place.z)]))
        own.append(links.here(("q", which, 1), src.at[SIDE], dst.at[:, cols(SIDE + mine)]))
    hot = slot_hot_of(assign)
    divisor = jnp.maximum(jnp.sum(hot, axis=1, keepdims=True), 1.0)
    hot = hot.astype(BF)

    def stage(kv, slot):
        first, count = GROUPS[slot]
        half_in, full_in, out = halves.at[kv, slot], fulls.at[kv, slot], outgoing.at[kv, slot]

        def term(step):
            y = shift(place.y, step)
            links.got(("s", kv, slot, step), twin.at[kv, slot, y])
            return parts[kv][slot, y, place.core].astype(F32) + twin[kv, slot, y].astype(F32)

        def start():
            out[2] = term(2).astype(BF)
            links.go(("h", kv, slot, 1), low(out.at[2]), half_in.at[0], place.ring("y", 1))
            links.go(("h", kv, slot, -1), high(out.at[2]), half_in.at[1], place.ring("y", -1))

        def relay():
            ahead = term(1)
            behind = term(-1)
            half = SIDE // 2
            links.got(("h", kv, slot, 1), half_in.at[0])
            out[0, 0:half] = (ahead[0:half] + half_in[0].astype(F32)).astype(BF)
            out[0, half:SIDE] = ahead[half:SIDE].astype(BF)
            links.go(("y", kv, slot, 1), out.at[0], full_in.at[0], place.ring("y", 1))
            links.got(("h", kv, slot, -1), half_in.at[1])
            out[1, 0:half] = behind[0:half].astype(BF)
            out[1, half:SIDE] = (behind[half:SIDE] + half_in[1].astype(F32)).astype(BF)
            links.go(("y", kv, slot, -1), out.at[1], full_in.at[1], place.ring("y", -1))

        def row():
            total = term(0)
            links.got(("y", kv, slot, 1), full_in.at[0])
            links.got(("y", kv, slot, -1), full_in.at[1])
            total = total + full_in[0].astype(F32) + full_in[1].astype(F32)
            column[kv, slot] = total.astype(BF)
            for step in STEPS:
                links.go(
                    ("z", kv, slot, step), column.at[kv, slot, shift(place.z, step)],
                    pieces.at[kv, slot, place.z], place.ring("z", step),
                )
            pieces[kv, slot, place.z] = column[kv, slot, place.z]

        def expand():
            for step in STEPS:
                links.got(("z", kv, slot, step), pieces.at[kv, slot, shift(place.z, -step)])
            ready = [pieces[kv, slot, z].astype(F32) for z in range(SIDE)]
            if slot == 1:
                ready = [ready[0] + ready[1], ready[2] + ready[3]]
            mean = jnp.concatenate([(one / divisor).astype(BF) for one in ready], axis=1)
            tokens[kv, :, first * HD : (first + count) * HD] = lax.dot_general(
                hot, mean, (((0,), (0,)), ((), ())), preferred_element_type=F32
            ).astype(BF)
            to = cols(place.x * HEADS_X + first, count)
            for step in STEPS:
                links.go(
                    ("x", kv, slot, step),
                    tokens.at[kv, token_rows(shift(place.x, step)), cols(first, count)],
                    outs[kv].at[:, to],
                    place.ring("x", step),
                )
            own.append(
                links.here(
                    ("x", kv, slot),
                    tokens.at[kv, token_rows(place.x), cols(first, count)],
                    outs[kv].at[:, to],
                )
            )

        return [start, relay, row, expand]

    run_rounds([stage(kv, slot) for kv, slot in PARTS], 1)

    for which, dst in enumerate((attended, query_grad)):
        for step in STEPS:
            links.got(("q", which, step), dst.at[:, cols(shift(place.z, -step))])
        links.got(("q", which, "partner"), dst.at[:, cols(SIDE + 1 - mine)])
    for kv, slot in PARTS:
        first, count = GROUPS[slot]
        for step in STEPS:
            links.got(
                ("x", kv, slot, step),
                outs[kv].at[:, cols(shift(place.x, -step) * HEADS_X + first, count)],
            )
    for copy in own:
        copy.wait()
    links.finish()


ANY = pl.BlockSpec(memory_space=pl.ANY)
VMEM = pl.BlockSpec(memory_space=pltpu.VMEM)
SMEM = pl.BlockSpec(memory_space=pltpu.SMEM)
ALL_FRAMES = SIDE * SIDE * CORES


def body(queries, keys_in, values_in, grad_out, assign, pattern, live_blocks):
    assign_rows = jnp.broadcast_to(assign[None, :], (8, TOK))
    shape = jax.ShapeDtypeStruct
    dma = pltpu.SemaphoreType.DMA
    spread = (2, SIDE, CORES, SIDE, SLOTS, HD)
    every_key, every_value, query_units, upstream_units = pl.pallas_call(
        gather_kernel,
        out_shape=(
            shape(spread, BF),
            shape(spread, BF),
            shape((UNITS, TOK, HD), BF),
            shape((UNITS, TOK, HD), BF),
        ),
        in_specs=[ANY, ANY, ANY, ANY, VMEM],
        out_specs=(VMEM, VMEM, ANY, ANY),
        scratch_shapes=[
            pltpu.VMEM((2, TOK, WIDTH), BF),
            pltpu.VMEM((2, HEADS_X, SLOTS, HD), BF),
            dma((GATHER_SEMS,)),
            dma((GATHER_SEMS,)),
            dma((GATHER_LOCAL,)),
        ],
        compiler_params=pltpu.CompilerParams(
            collective_id=0, has_side_effects=True, vmem_limit_bytes=VMEM_LIMIT
        ),
        name="gather",
    )(keys_in, values_in, queries, grad_out, assign_rows)

    blocks = (2, ALL_FRAMES * SLOTS // KB, KB, HD)

    def head_block():
        return pl.BlockSpec((1,) + blocks[1:], lambda u: (u // SIDE, 0, 0, 0))

    def token_block():
        return pl.BlockSpec((1, TOK, HD), lambda u: (u, 0, 0))

    att_units, dq_units, key_part, value_part = pl.pallas_call(
        attention_kernel,
        grid=(UNITS,),
        out_shape=(
            shape((UNITS, TOK, HD), BF),
            shape((UNITS, TOK, HD), BF),
            shape(blocks, BF),
            shape(blocks, BF),
        ),
        in_specs=[SMEM, SMEM, head_block(), head_block(), token_block(), token_block()],
        out_specs=(token_block(), token_block(), head_block(), head_block()),
        scratch_shapes=[
            pltpu.VMEM((NSEL * KB, HD), BF),
            pltpu.VMEM((NSEL * KB, HD), BF),
            pltpu.VMEM((NSEL * KB, TOK), F32),
            pltpu.VMEM((NSEL * KB, HD), F32),
            pltpu.VMEM((NSEL * KB, HD), F32),
        ],
        compiler_params=pltpu.CompilerParams(vmem_limit_bytes=VMEM_LIMIT),
        name="attention",
    )(
        pattern, live_blocks, every_key.reshape(blocks), every_value.reshape(blocks),
        query_units, upstream_units,
    )

    return pl.pallas_call(
        scatter_kernel,
        out_shape=(
            shape(queries.shape, BF),
            shape(queries.shape, BF),
            shape(keys_in.shape, BF),
            shape(keys_in.shape, BF),
        ),
        in_specs=[VMEM, VMEM, ANY, ANY, VMEM],
        out_specs=(ANY, ANY, ANY, ANY),
        scratch_shapes=[
            pltpu.VMEM((2, 2, SIDE, SIDE, SLOTS, HD), BF),
            pltpu.VMEM((2, 2, 2, SIDE // 2, SLOTS, HD), BF),
            pltpu.VMEM((2, 2, 2, SIDE, SLOTS, HD), BF),
            pltpu.VMEM((2, 2, 3, SIDE, SLOTS, HD), BF),
            pltpu.VMEM((2, 2, SIDE, SLOTS, HD), BF),
            pltpu.VMEM((2, 2, SIDE, SLOTS, HD), BF),
            pltpu.VMEM((2, TOK, WIDTH), BF),
            dma((SCATTER_SEMS,)),
            dma((SCATTER_SEMS,)),
            dma((SCATTER_LOCAL,)),
        ],
        compiler_params=pltpu.CompilerParams(
            collective_id=1, has_side_effects=True, vmem_limit_bytes=VMEM_LIMIT
        ),
        name="scatter",
    )(key_part.reshape(spread), value_part.reshape(spread), att_units, dq_units, assign_rows)


def solution(mesh):
    return jax.shard_map(
        body,
        mesh=mesh,
        in_specs=(
            P("frame", "head"),
            P(("frame", "head"), None),
            P(("frame", "head"), None),
            P("frame", "head"),
            P("frame"),
            P(),
            P(),
        ),
        out_specs=(
            P("frame", "head"),
            P("frame", "head"),
            P(("frame", "head"), None),
            P(("frame", "head"), None),
        ),
        check_vma=False,
    )
```

profile of v0, /device:TPU:24, one launch (start us, length us, event | category | flops | bytes accessed | tf_op | source)
XLA Modules:
  0.0 135.3 jit_solution(5961422005245323388)
XLA Ops:
  0.6 1.3 broadcast_in_dim.2.assign
  1.9 1.4 %copy.11.pattern = s32[32,16]{1,0:T(8,128)} copy(s32[32,16]{0,1:T(8,128)} %param.12) | data formatting | bytes 4096 | tf_op args[5]
  3.3 51.3 %gather.1 = (bf16[2,4,2,4,128,128]{5,4,3,2,1,0:T(8,128)(2,1)}, bf16[2,4,2,4,128,128]{5,4,3,2,1,0:T(8,128)(2,1)}, bf16[6,512,128]{2,1,0:T(8,128)(2,1)}, bf16[6,512,128]{2,1,0:T(8,128)(2,1)}) custom-call(bf16[128,3072]{1,0:T(8,128)(2,1)} %keys.1, bf16[128,3072]{1,0:T(8,128)(2,1)} %values.1, bf16[512,768]{1,0:T(8,128)(2,1)} %queries.1, ...), custom_call_target="tpu_custom_call" | custom-call | tf_op jit(solution)/shard_map/gather/pallas_call | solution.py:503
  54.6 20.9 %attention.1 = (bf16[6,512,128]{2,1,0:T(8,128)(2,1)}, bf16[6,512,128]{2,1,0:T(8,128)(2,1)}, bf16[2,64,64,128]{3,2,1,0:T(8,128)(2,1)}, bf16[2,64,64,128]{3,2,1,0:T(8,128)(2,1)}) custom-call(s32[32,16]{1,0:T(8,128)} %copy.11.pattern, s32[32]{0:T(128)} %live.1, bf16[2,64,64,128]{3,2,1,0:T(8,128)(2,1)} %bitcast.4, bf16[2,64,64,128]{3,2,1,0:T(8,128)(2,1)} %bitcast.5, ...), custom_call_target="tpu_custom_call" | custom-call | tf_op jit(solution)/shard_map/attention/pallas_call | solution.py:534
  75.5 54.9 %scatter.1 = (bf16[512,768]{1,0:T(8,128)(2,1)}, bf16[512,768]{1,0:T(8,128)(2,1)}, bf16[128,3072]{1,0:T(8,128)(2,1)}, bf16[128,3072]{1,0:T(8,128)(2,1)}) custom-call(bf16[2,4,2,4,128,128]{5,4,3,2,1,0:T(8,128)(2,1)} %bitcast.6, bf16[2,4,2,4,128,128]{5,4,3,2,1,0:T(8,128)(2,1)} %bitcast.7, bf16[6,512,128]{2,1,0:T(8,128)(2,1)} %get-tuple-element.18.att_in, ...), custom_call_target="tpu_custom_call" | custom-call | tf_op jit(solution)/shard_map/scatter/pallas_call | solution.py:559
  130.4 0.0 copy-start.2
  130.4 0.0 copy-start.1
  130.5 0.0 copy-start
  130.5 2.2 %copy.16 = bf16[512,768]{1,0:T(8,128)(2,1)} copy(bf16[512,768]{1,0:T(8,128)(2,1)} %get-tuple-element.24) | data formatting | bytes 1572864
  132.7 0.0 copy-done.2
  132.7 0.9 copy.17
  133.6 0.0 copy-done.1
  133.6 0.9 copy.18
  134.4 0.0 copy-done
  134.5 0.9 copy.19
Async XLA Ops:
  130.4 2.2 %copy-start.2 = (bf16[512,768]{1,0:T(8,128)(2,1)S(1)}, bf16[512,768]{1,0:T(8,128)(2,1)}, u32[]{:S(2)}) copy-start(bf16[512,768]{1,0:T(8,128)(2,1)} %get-tuple-element.25) | copy-start | bytes 2359300
  130.4 3.1 %copy-start.1 = (bf16[128,3072]{1,0:T(8,128)(2,1)S(1)}, bf16[128,3072]{1,0:T(8,128)(2,1)}, u32[]{:S(2)}) copy-start(bf16[128,3072]{1,0:T(8,128)(2,1)} %get-tuple-element.26) | copy-start | bytes 2359300
  130.5 4.0 %copy-start = (bf16[128,3072]{1,0:T(8,128)(2,1)S(1)}, bf16[128,3072]{1,0:T(8,128)(2,1)}, u32[]{:S(2)}) copy-start(bf16[128,3072]{1,0:T(8,128)(2,1)} %get-tuple-element.27) | copy-start | bytes 2359300
where the time goes:
time: 136 us; the launch traced here: 135 us
  Pallas kernels  127 us (93%)
  local copies, waits for them, and re-layouts  7.53 us (6%)
    pallas_call x1, Pallas kernels, body(): pl.pallas_call(scatter_kernel, out_shape=(shape(queries.shape, BF), shape...  54.9 us
    pallas_call x1, Pallas kernels, body(): pl.pallas_call(gather_kernel, out_shape=(shape(spread, BF), shape(spread,...  51.3 us
    pallas_call x1, Pallas kernels, body(): pl.pallas_call(attention_kernel, grid=(UNITS,), out_shape=(shape((UNITS,...  20.9 us
    unnamed x11, local copies, waits for them, and re-layouts  6.24 us

commit v1 on v0

--- a/solution.py
+++ b/solution.py
@@ -1,3 +1,4 @@
+import functools
 import math
 
 import jax
@@ -10,6 +11,7 @@
 HD = 128
 KB = 64
 NSEL = 16
+SIZES = (256, 512, 768, 1024)
 SIDE = 4
 CORES = 2
 HEADS_X = 6
@@ -18,15 +20,19 @@
 TOK_DEV = TOK // SIDE
 SLOTS = 128
 UNITS = 6
-CHUNK = 256
+CHUNK = 512
 SCALE = 1.0 / math.sqrt(HD)
 MESH = pl.DeviceIdType.MESH
 BF = jnp.bfloat16
 F32 = jnp.float32
-VMEM_LIMIT = 56 * 1024 * 1024
+VMEM_LIMIT = 20 * 1024 * 1024
+LOG2_E = math.log2(math.e)
 STEPS = (1, -1, 2)
 GROUPS = ((0, SIDE), (SIDE, HEADS_X - SIDE))
-PARTS = ((0, 0), (1, 0), (0, 1), (1, 1))
+GATHER_PARTS = ((0, 1), (1, 1), (0, 0), (1, 0))
+SCATTER_PARTS = ((1, 0), (0, 0), (1, 1), (0, 1))
+GATHER_STRAIGHT = GATHER_PARTS[2:]
+SCATTER_STRAIGHT = SCATTER_PARTS[:1]
 
 
 class Place:
@@ -58,8 +64,7 @@
 
 def meet(place):
     partners = [place.sibling()]
-    partners += [place.ring(axis, step) for axis in ("x", "z") for step in STEPS]
-    partners += [place.ring("y", step) for step in (1, -1)]
+    partners += [place.ring(axis, step) for axis in ("x", "y", "z") for step in STEPS]
     barrier = pltpu.get_barrier_semaphore()
     for target in partners:
         pl.semaphore_signal(barrier, inc=1, device_id=target, device_id_type=MESH)
@@ -138,8 +143,8 @@
             step()
 
 
-GATHER_SEMS = len(PARTS) * 14 + 2 * 4
-GATHER_LOCAL = len(PARTS) + 4
+GATHER_SEMS = len(GATHER_PARTS) * 14 + 2 * 4
+GATHER_LOCAL = len(GATHER_PARTS) + 4
 
 
 def gather_kernel(
@@ -186,11 +191,11 @@
             ("q", which, 1), src.at[:, cols(SIDE + mine)], dst.at[SIDE]
         )
 
-    send_tokens(*PARTS[0])
-    send_tokens(*PARTS[1])
+    send_tokens(*GATHER_PARTS[0])
+    send_tokens(*GATHER_PARTS[1])
     send_queries(0)
-    send_tokens(*PARTS[2])
-    send_tokens(*PARTS[3])
+    send_tokens(*GATHER_PARTS[2])
+    send_tokens(*GATHER_PARTS[3])
     hot = slot_hot_of(assign)
     divisor = jnp.maximum(jnp.sum(hot, axis=1, keepdims=True), 1.0)
     hot = hot.astype(BF)
@@ -198,6 +203,7 @@
     def stage(kv, slot):
         first, count = GROUPS[slot]
         out = every[kv]
+        straight = (kv, slot) in GATHER_STRAIGHT
 
         def region(step):
             return out.at[slot, shift(place.y, step), place.core]
@@ -230,7 +236,7 @@
                     place.ring("z", step),
                 )
             out[slot, place.y, place.core, place.z] = merged[kv, head_of(place.z)]
-            if (kv, slot) == PARTS[0]:
+            if (kv, slot) == GATHER_PARTS[0]:
                 send_queries(1)
 
         def row():
@@ -239,21 +245,26 @@
                     ("z", kv, slot, step),
                     out.at[slot, place.y, place.core, shift(place.z, -step)],
                 )
-            links.go(("y", kv, slot, 1), region(0), region(0), place.ring("y", 1))
-            links.go(("y", kv, slot, -1), region(0), region(0), place.ring("y", -1))
+            for step in STEPS if straight else STEPS[:2]:
+                links.go(("y", kv, slot, step), region(0), region(0), place.ring("y", step))
             pass_on(0)
 
         def near():
             links.got(("y", kv, slot, 1), region(-1))
-            links.go(("f", kv, slot, 1), low(region(-1)), low(region(-1)), place.ring("y", 1))
+            if not straight:
+                links.go(("f", kv, slot, 1), low(region(-1)), low(region(-1)), place.ring("y", 1))
             pass_on(-1)
             links.got(("y", kv, slot, -1), region(1))
-            links.go(("f", kv, slot, -1), high(region(1)), high(region(1)), place.ring("y", -1))
+            if not straight:
+                links.go(("f", kv, slot, -1), high(region(1)), high(region(1)), place.ring("y", -1))
             pass_on(1)
 
         def far():
-            links.got(("f", kv, slot, 1), low(region(2)))
-            links.got(("f", kv, slot, -1), high(region(2)))
+            if straight:
+                links.got(("y", kv, slot, 2), region(2))
+            else:
+                links.got(("f", kv, slot, 1), low(region(2)))
+                links.got(("f", kv, slot, -1), high(region(2)))
             pass_on(2)
 
         def close():
@@ -264,7 +275,7 @@
 
         return [merge, row, near, far, close]
 
-    run_rounds([stage(kv, slot) for kv, slot in PARTS], 1)
+    run_rounds([stage(kv, slot) for kv, slot in GATHER_PARTS], 1)
     for which, dst in enumerate((query_out, upstream_out)):
         for step in STEPS:
             links.got(("q", which, step), dst.at[shift(place.z, -step)])
@@ -277,91 +288,96 @@
 def attention_kernel(
     pattern, live, keys, values, query, upstream,
     attended, query_grad, key_grad, value_grad,
-    ksel, vsel, expo, kpart, vpart,
+    ksel, vsel, expo, prob_grad, kpart, vpart,
 ):
     place = Place()
-    unit = pl.program_id(0)
-    unit_z = jnp.where(unit < SIDE, unit, jnp.where(unit == SIDE, place.z, SIDE - 1 - place.z))
-    frame = (place.y * SIDE + unit_z) * CORES + place.core
-    count = live[frame]
-    chunks = (count * KB + CHUNK - 1) // CHUNK
-    rows_live = count * KB
+    key_grad[...] = jnp.zeros_like(key_grad)
+    value_grad[...] = jnp.zeros_like(value_grad)
 
     def spot_of(block):
         owner = block // 2
         y, z, core = owner // (CORES * SIDE), (owner // CORES) % SIDE, owner % CORES
         return ((y * CORES + core) * SIDE + z) * 2 + block % 2
 
-    @pl.when((unit == 0) | (unit == SIDE))
-    def _():
-        key_grad[...] = jnp.zeros_like(key_grad)
-        value_grad[...] = jnp.zeros_like(value_grad)
-
-    for j in range(NSEL):
-        spot = spot_of(pattern[frame, j])
-        ksel[pl.ds(j * KB, KB), :] = keys[0, spot]
-        vsel[pl.ds(j * KB, KB), :] = values[0, spot]
-    q = query[0]
-    g = upstream[0]
-    q_t = q.T
-    g_t = g.T
-
-    def rows_of(c):
-        return pl.ds(pl.multiple_of(c * CHUNK, CHUNK), CHUNK)
-
-    def score_step(c, top):
-        scores = jnp.dot(ksel[rows_of(c), :], q_t, preferred_element_type=F32) * SCALE
-        ids = lax.broadcasted_iota(jnp.int32, (CHUNK, TOK), 0) + c * CHUNK
-        scores = jnp.where(ids < rows_live, scores, -jnp.inf)
-        expo[rows_of(c), :] = scores
-        return jnp.maximum(top, jnp.max(scores, axis=0, keepdims=True))
-
-    top = lax.fori_loop(0, chunks, score_step, jnp.full((1, TOK), -jnp.inf, F32))
-
-    def value_step(c, state):
-        total, weighted = state
-        weights = jnp.exp(expo[rows_of(c), :] - top)
-        expo[rows_of(c), :] = weights
-        total = total + jnp.sum(weights, axis=0, keepdims=True)
-        weighted = weighted + lax.dot_general(
-            vsel[rows_of(c), :], weights.astype(BF), (((0,), (0,)), ((), ())),
-            preferred_element_type=F32,
-        )
-        return total, weighted
-
-    total, weighted = lax.fori_loop(
-        0, chunks, value_step, (jnp.zeros((1, TOK), F32), jnp.zeros((HD, TOK), F32))
-    )
-    att_t = (weighted / total).astype(BF)
-    attended[0] = att_t.T
-    delta = jnp.sum(g_t.astype(F32) * att_t.astype(F32), axis=0, keepdims=True)
-    inverse = 1.0 / total
-
-    def grad_step(c, dq):
-        probs = expo[rows_of(c), :] * inverse
-        prob_grad = jnp.dot(vsel[rows_of(c), :], g_t, preferred_element_type=F32)
-        score_grad = (probs * (prob_grad - delta)).astype(BF)
-        kpart[rows_of(c), :] = jnp.dot(score_grad, q, preferred_element_type=F32) * SCALE
-        vpart[rows_of(c), :] = jnp.dot(probs.astype(BF), g, preferred_element_type=F32)
-        return dq + lax.dot_general(
-            ksel[rows_of(c), :], score_grad, (((0,), (0,)), ((), ())), preferred_element_type=F32
-        )
-
-    dq = lax.fori_loop(0, chunks, grad_step, jnp.zeros((HD, TOK), F32))
-    query_grad[0] = (dq * SCALE).astype(BF).T
-
-    for j in range(NSEL):
-
-        @pl.when(j < count)
-        def _():
-            spot = spot_of(pattern[frame, j])
-            for out, part in ((key_grad, kpart), (value_grad, vpart)):
-                piece = part[pl.ds(j * KB, KB), :].astype(BF).astype(F32)
-                out[0, spot] = (out[0, spot].astype(F32) + piece).astype(BF)
-
-
-SCATTER_SEMS = len(PARTS) * 14 + 2 * 4
-SCATTER_LOCAL = len(PARTS) + 4
+    def unit_step(unit, carry):
+        slot = unit // SIDE
+        unit_z = jnp.where(unit < SIDE, unit, jnp.where(unit == SIDE, place.z, SIDE - 1 - place.z))
+        frame = (place.y * SIDE + unit_z) * CORES + place.core
+        count = live[frame]
+        rows_live = count * KB
+
+        def attend(least, rows):
+            for j in range(rows // KB):
+                spot = spot_of(pattern[j, frame])
+                ksel[j * KB : (j + 1) * KB, :] = keys[slot, spot]
+                vsel[j * KB : (j + 1) * KB, :] = values[slot, spot]
+            q, g = query[unit], upstream[unit]
+            q_t, g_t = q.T, g.T
+            spans = [(a, min(a + CHUNK, rows)) for a in range(0, rows, CHUNK)]
+            top = jnp.full((1, TOK), -jnp.inf, F32)
+            for a, b in spans:
+                scores = jnp.dot(ksel[a:b, :], q_t, preferred_element_type=F32)
+                if b > least:
+                    ids = lax.broadcasted_iota(jnp.int32, (b - a, TOK), 0) + a
+                    scores = jnp.where(ids < rows_live, scores, -jnp.inf)
+                expo[a:b, :] = scores
+                top = jnp.maximum(top, jnp.max(scores, axis=0, keepdims=True))
+                prob_grad[a:b, :] = jnp.dot(vsel[a:b, :], g_t, preferred_element_type=F32)
+            top = top * (SCALE * LOG2_E)
+            total = jnp.zeros((1, TOK), F32)
+            weighted = jnp.zeros((HD, TOK), F32)
+            for a, b in spans:
+                weights = jnp.exp2(expo[a:b, :] * (SCALE * LOG2_E) - top)
+                expo[a:b, :] = weights
+                total = total + jnp.sum(weights, axis=0, keepdims=True)
+                weighted = weighted + lax.dot_general(
+                    vsel[a:b, :], weights.astype(BF), (((0,), (0,)), ((), ())),
+                    preferred_element_type=F32,
+                )
+            inverse = 1.0 / total
+            att_t = (weighted * inverse).astype(BF)
+            attended[unit] = att_t.T
+            delta = jnp.sum(g_t.astype(F32) * att_t.astype(F32), axis=0, keepdims=True)
+            dq = jnp.zeros((HD, TOK), F32)
+            for a, b in spans:
+                probs = expo[a:b, :] * inverse
+                score_grad = (probs * (prob_grad[a:b, :] - delta)).astype(BF)
+                kpart[a:b, :] = (
+                    jnp.dot(score_grad, q, preferred_element_type=F32) * SCALE
+                ).astype(BF)
+                vpart[a:b, :] = jnp.dot(
+                    probs.astype(BF), g, preferred_element_type=F32
+                ).astype(BF)
+                dq = dq + lax.dot_general(
+                    ksel[a:b, :], score_grad, (((0,), (0,)), ((), ())), preferred_element_type=F32
+                )
+            query_grad[unit] = (dq * SCALE).astype(BF).T
+            for j in range(rows // KB):
+
+                def add(j=j):
+                    spot = spot_of(pattern[j, frame])
+                    for out, part in ((key_grad, kpart), (value_grad, vpart)):
+                        piece = part[j * KB : (j + 1) * KB, :].astype(F32)
+                        out[slot, spot] = (out[slot, spot].astype(F32) + piece).astype(BF)
+
+                if j * KB < least:
+                    add()
+                else:
+                    pl.when(j < count)(add)
+
+        least = 0
+        for rows in SIZES:
+            pl.when((rows_live > least) & (rows_live <= rows))(
+                functools.partial(attend, least, rows)
+            )
+            least = rows
+        return carry
+
+    lax.fori_loop(0, UNITS, unit_step, 0)
+
+
+SCATTER_SEMS = len(SCATTER_PARTS) * 14 + 2 * 4
+SCATTER_LOCAL = len(SCATTER_PARTS) + 4
 
 
 def scatter_kernel(
@@ -384,7 +400,7 @@
                 twin.at[kv, slot, y], place.sibling(),
             )
 
-    for kv, slot in PARTS:
+    for kv, slot in SCATTER_PARTS:
         send_twin(kv, slot)
     mine = place.z // 2
     for which, (src, dst) in enumerate(((att_in, attended), (dq_in, query_grad))):
@@ -405,6 +421,7 @@
 
     def stage(kv, slot):
         first, count = GROUPS[slot]
+        straight = (kv, slot) in SCATTER_STRAIGHT
         half_in, full_in, out = halves.at[kv, slot], fulls.at[kv, slot], outgoing.at[kv, slot]
 
         def term(step):
@@ -414,6 +431,9 @@
 
         def start():
             out[2] = term(2).astype(BF)
+            if straight:
+                links.go(("y", kv, slot, 2), out.at[2], full_in.at[2], place.ring("y", 2))
+                return
             links.go(("h", kv, slot, 1), low(out.at[2]), half_in.at[0], place.ring("y", 1))
             links.go(("h", kv, slot, -1), high(out.at[2]), half_in.at[1], place.ring("y", -1))
 
@@ -421,6 +441,13 @@
             ahead = term(1)
             behind = term(-1)
             half = SIDE // 2
+            if straight:
+                for at, step, value in ((0, 1, ahead), (1, -1, behind)):
+                    out[at] = value.astype(BF)
+                    links.go(
+                        ("y", kv, slot, step), out.at[at], full_in.at[at], place.ring("y", step)
+                    )
+                return
             links.got(("h", kv, slot, 1), half_in.at[0])
             out[0, 0:half] = (ahead[0:half] + half_in[0].astype(F32)).astype(BF)
             out[0, half:SIDE] = ahead[half:SIDE].astype(BF)
@@ -435,6 +462,9 @@
             links.got(("y", kv, slot, 1), full_in.at[0])
             links.got(("y", kv, slot, -1), full_in.at[1])
             total = total + full_in[0].astype(F32) + full_in[1].astype(F32)
+            if straight:
+                links.got(("y", kv, slot, 2), full_in.at[2])
+                total = total + full_in[2].astype(F32)
             column[kv, slot] = total.astype(BF)
             for step in STEPS:
                 links.go(
@@ -471,13 +501,13 @@
 
         return [start, relay, row, expand]
 
-    run_rounds([stage(kv, slot) for kv, slot in PARTS], 1)
+    run_rounds([stage(kv, slot) for kv, slot in SCATTER_PARTS], 1)
 
     for which, dst in enumerate((attended, query_grad)):
         for step in STEPS:
             links.got(("q", which, step), dst.at[:, cols(shift(place.z, -step))])
         links.got(("q", which, "partner"), dst.at[:, cols(SIDE + 1 - mine)])
-    for kv, slot in PARTS:
+    for kv, slot in SCATTER_PARTS:
         first, count = GROUPS[slot]
         for step in STEPS:
             links.got(
@@ -490,13 +520,14 @@
 
 
 ANY = pl.BlockSpec(memory_space=pl.ANY)
+HBM = pl.BlockSpec(memory_space=pltpu.HBM)
 VMEM = pl.BlockSpec(memory_space=pltpu.VMEM)
 SMEM = pl.BlockSpec(memory_space=pltpu.SMEM)
 ALL_FRAMES = SIDE * SIDE * CORES
 
 
 def body(queries, keys_in, values_in, grad_out, assign, pattern, live_blocks):
-    assign_rows = jnp.broadcast_to(assign[None, :], (8, TOK))
+    assign_rows = assign.reshape(1, TOK)
     shape = jax.ShapeDtypeStruct
     dma = pltpu.SemaphoreType.DMA
     spread = (2, SIDE, CORES, SIDE, SLOTS, HD)
@@ -508,8 +539,8 @@
             shape((UNITS, TOK, HD), BF),
             shape((UNITS, TOK, HD), BF),
         ),
-        in_specs=[ANY, ANY, ANY, ANY, VMEM],
-        out_specs=(VMEM, VMEM, ANY, ANY),
+        in_specs=[HBM, HBM, HBM, HBM, VMEM],
+        out_specs=(VMEM, VMEM, VMEM, VMEM),
         scratch_shapes=[
             pltpu.VMEM((2, TOK, WIDTH), BF),
             pltpu.VMEM((2, HEADS_X, SLOTS, HD), BF),
@@ -525,34 +556,28 @@
 
     blocks = (2, ALL_FRAMES * SLOTS // KB, KB, HD)
 
-    def head_block():
-        return pl.BlockSpec((1,) + blocks[1:], lambda u: (u // SIDE, 0, 0, 0))
-
-    def token_block():
-        return pl.BlockSpec((1, TOK, HD), lambda u: (u, 0, 0))
-
     att_units, dq_units, key_part, value_part = pl.pallas_call(
         attention_kernel,
-        grid=(UNITS,),
         out_shape=(
             shape((UNITS, TOK, HD), BF),
             shape((UNITS, TOK, HD), BF),
             shape(blocks, BF),
             shape(blocks, BF),
         ),
-        in_specs=[SMEM, SMEM, head_block(), head_block(), token_block(), token_block()],
-        out_specs=(token_block(), token_block(), head_block(), head_block()),
+        in_specs=[SMEM, SMEM, VMEM, VMEM, VMEM, VMEM],
+        out_specs=(VMEM, VMEM, VMEM, VMEM),
         scratch_shapes=[
             pltpu.VMEM((NSEL * KB, HD), BF),
             pltpu.VMEM((NSEL * KB, HD), BF),
             pltpu.VMEM((NSEL * KB, TOK), F32),
-            pltpu.VMEM((NSEL * KB, HD), F32),
-            pltpu.VMEM((NSEL * KB, HD), F32),
+            pltpu.VMEM((NSEL * KB, TOK), F32),
+            pltpu.VMEM((NSEL * KB, HD), BF),
+            pltpu.VMEM((NSEL * KB, HD), BF),
         ],
         compiler_params=pltpu.CompilerParams(vmem_limit_bytes=VMEM_LIMIT),
         name="attention",
     )(
-        pattern, live_blocks, every_key.reshape(blocks), every_value.reshape(blocks),
+        pattern.T, live_blocks, every_key.reshape(blocks), every_value.reshape(blocks),
         query_units, upstream_units,
     )
 
@@ -564,12 +589,12 @@
             shape(keys_in.shape, BF),
             shape(keys_in.shape, BF),
         ),
-        in_specs=[VMEM, VMEM, ANY, ANY, VMEM],
+        in_specs=[VMEM, VMEM, VMEM, VMEM, VMEM],
         out_specs=(ANY, ANY, ANY, ANY),
         scratch_shapes=[
             pltpu.VMEM((2, 2, SIDE, SIDE, SLOTS, HD), BF),
             pltpu.VMEM((2, 2, 2, SIDE // 2, SLOTS, HD), BF),
-            pltpu.VMEM((2, 2, 2, SIDE, SLOTS, HD), BF),
+            pltpu.VMEM((2, 2, 3, SIDE, SLOTS, HD), BF),
             pltpu.VMEM((2, 2, 3, SIDE, SLOTS, HD), BF),
             pltpu.VMEM((2, 2, SIDE, SLOTS, HD), BF),
             pltpu.VMEM((2, 2, SIDE, SLOTS, HD), BF),

time: 136 us -> 115 us (0.85)
  the two profiles are of different devices: /device:TPU:24 before, /device:TPU:0 now
where the time goes in v1:
time: 115 us; the launch traced here: 114 us
  Pallas kernels  105 us (91%)
  local copies, waits for them, and re-layouts  8.74 us (8%)
    pallas_call x1, Pallas kernels, body(): pl.pallas_call(gather_kernel, out_shape=(shape(spread, BF), shape(spread,...  50.1 us
    pallas_call x1, Pallas kernels, body(): pl.pallas_call(scatter_kernel, out_shape=(shape(queries.shape, BF), shape...  44.1 us
    pallas_call x1, Pallas kernels, body(): pl.pallas_call(attention_kernel, out_shape=(shape((UNITS, TOK, HD), BF),...  10.9 us
    unnamed x18, local copies, waits for them, and re-layouts  8.74 us

profile of v1, /device:TPU:0, one launch (start us, length us, event | category | flops | bytes accessed | tf_op | source)
XLA Modules:
  0.0 114.4 jit_solution(1888384302653013175)
XLA Ops:
  0.6 0.0 copy-start.6
  0.6 0.0 copy-start
  0.7 1.1 copy-done
  1.8 0.0 copy-start.1
  1.8 1.1 copy-done.1
  2.9 0.0 copy-start.2
  2.9 1.1 copy-done.2
  4.1 0.0 copy-start.3
  4.1 1.1 copy-done.3
  5.2 0.0 copy-start.5
  5.2 0.7 copy-done.5
  5.9 0.0 copy-start.4
  5.9 50.1 %gather.1 = (bf16[2,4,2,4,128,128]{5,4,3,2,1,0:T(8,128)(2,1)S(1)}, bf16[2,4,2,4,128,128]{5,4,3,2,1,0:T(8,128)(2,1)S(1)}, bf16[6,512,128]{2,1,0:T(8,128)(2,1)S(1)}, bf16[6,512,128]{2,1,0:T(8,128)(2,1)S(1)}) custom-call(bf16[128,3072]{1,0:T(8,128)(2,1)S(1)} %copy-done, bf16[128,3072]{1,0:T(8,128)(2,1)S(1)} %copy-done.1, bf16[512,768]{1,0:T(8,128)(2,1)S(1)} %copy-done.2, ...), custom_call_target="tpu_custom_call" | custom-call | tf_op jit(solution)/shard_map/gather/pallas_call | solution.py:534
  55.9 0.0 copy-done.6
  56.0 0.0 copy-done.4
  56.0 10.9 %attention.1 = (bf16[6,512,128]{2,1,0:T(8,128)(2,1)S(1)}, bf16[6,512,128]{2,1,0:T(8,128)(2,1)S(1)}, bf16[2,64,64,128]{3,2,1,0:T(8,128)(2,1)S(1)}, bf16[2,64,64,128]{3,2,1,0:T(8,128)(2,1)S(1)}) custom-call(s32[16,32]{1,0:T(8,128)S(1)} %bitcast.10, s32[32]{0:T(128)S(1)} %copy-done.6, bf16[2,64,64,128]{3,2,1,0:T(8,128)(2,1)S(1)} %bitcast.8, ...), custom_call_target="tpu_custom_call" | custom-call | tf_op jit(solution)/shard_map/attention/pallas_call | solution.py:559
  66.8 44.1 %scatter.1 = (bf16[512,768]{1,0:T(8,128)(2,1)S(1)}, bf16[512,768]{1,0:T(8,128)(2,1)S(1)}, bf16[128,3072]{1,0:T(8,128)(2,1)S(1)}, bf16[128,3072]{1,0:T(8,128)(2,1)S(1)}) custom-call(bf16[2,4,2,4,128,128]{5,4,3,2,1,0:T(8,128)(2,1)S(1)} %bitcast.6, bf16[2,4,2,4,128,128]{5,4,3,2,1,0:T(8,128)(2,1)S(1)} %bitcast.7, ...), custom_call_target="tpu_custom_call" | custom-call | tf_op jit(solution)/shard_map/scatter/pallas_call | solution.py:584
  110.9 0.9 copy.15
  111.8 0.9 copy.16
  112.7 0.9 copy.17
  113.5 0.9 copy.18
Async XLA Ops:
  0.6 55.3 %copy-start.6 = (s32[32]{0:T(128)S(1)}, s32[32]{0:T(128)}, u32[]{:S(2)}) copy-start(s32[32]{0:T(128)} %live.1) | copy-start | bytes 388
  0.6 1.1 copy-start
  1.8 1.1 copy-start.1
  2.9 1.1 copy-start.2
  4.1 1.1 copy-start.3
  5.2 0.7 copy-start.5
  5.9 50.1 %copy-start.4 = (s32[32,16]{0,1:T(8,128)S(1)}, s32[32,16]{0,1:T(8,128)}, u32[]{:S(2)}) copy-start(s32[32,16]{0,1:T(8,128)} %param.12) | copy-start | bytes 6148

commit v2 on v1

--- a/solution.py
+++ b/solution.py
@@ -31,7 +31,7 @@
 GROUPS = ((0, SIDE), (SIDE, HEADS_X - SIDE))
 GATHER_PARTS = ((0, 1), (1, 1), (0, 0), (1, 0))
 SCATTER_PARTS = ((1, 0), (0, 0), (1, 1), (0, 1))
-GATHER_STRAIGHT = GATHER_PARTS[2:]
+GATHER_STRAIGHT = GATHER_PARTS[3:]
 SCATTER_STRAIGHT = SCATTER_PARTS[:1]
 
 
@@ -54,8 +54,11 @@
     def sibling(self):
         return self.device(self.y, self.z, 1 - self.core, self.x)
 
+    def partner_z(self):
+        return jnp.where(self.core == 0, self.z + 1 - 2 * (self.z % 2), SIDE - 1 - self.z)
+
     def partner(self):
-        return self.device(self.y, SIDE - 1 - self.z, self.core, self.x)
+        return self.device(self.y, self.partner_z(), self.core, self.x)
 
 
 def shift(at, step):
@@ -133,24 +136,27 @@
     return (slots == assign[0:1, :]).astype(F32)
 
 
-def run_rounds(stages, stagger):
-    ticks = {}
-    for i, rounds in enumerate(stages):
-        for r, step in enumerate(rounds):
-            ticks.setdefault(i * stagger + r, []).append((-i, step))
-    for tick in sorted(ticks):
-        for _, step in sorted(ticks[tick], key=lambda item: item[0]):
-            step()
+MERGE, ROW, NEAR, FAR, CLOSE = range(5)
+GATHER_ORDER = (
+    (0, MERGE), (1, MERGE), (0, ROW), (1, ROW), (2, MERGE), (0, NEAR), (1, NEAR), (2, ROW), (0, FAR),
+    (3, MERGE), (1, FAR), (3, ROW), (2, NEAR), (2, FAR), (3, NEAR), (3, FAR),
+    (0, CLOSE), (1, CLOSE), (2, CLOSE), (3, CLOSE),
+)
+START, RELAY, TOTAL, EXPAND = range(4)
+SCATTER_ORDER = (
+    (0, START), (1, START), (2, START), (3, START), (0, RELAY), (1, RELAY), (2, RELAY), (3, RELAY),
+    (0, TOTAL), (0, EXPAND), (1, TOTAL), (1, EXPAND), (2, TOTAL), (2, EXPAND), (3, TOTAL), (3, EXPAND),
+)
 
 
 GATHER_SEMS = len(GATHER_PARTS) * 14 + 2 * 4
-GATHER_LOCAL = len(GATHER_PARTS) + 4
+GATHER_LOCAL = len(GATHER_PARTS) + 5
 
 
 def gather_kernel(
     keys, values, queries, upstream, assign,
     every_key, every_value, query_out, upstream_out,
-    tokens, merged, send, recv, local,
+    tokens, merged, assign_own, send, recv, local,
 ):
     place = Place()
     meet(place)
@@ -181,7 +187,7 @@
                 ("q", which, step), src.at[:, cols(shift(place.z, step))], dst.at[place.z],
                 place.ring("z", step),
             )
-        mine = place.z // 2
+        mine = place.z % 2
         links.go(
             ("q", which, "partner"), src.at[:, cols(SIDE + 1 - mine)], dst.at[SIDE + 1],
             place.partner(),
@@ -196,7 +202,8 @@
     send_queries(0)
     send_tokens(*GATHER_PARTS[2])
     send_tokens(*GATHER_PARTS[3])
-    hot = slot_hot_of(assign)
+    links.here("assign", assign, assign_own).wait()
+    hot = slot_hot_of(assign_own)
     divisor = jnp.maximum(jnp.sum(hot, axis=1, keepdims=True), 1.0)
     hot = hot.astype(BF)
 
@@ -226,7 +233,7 @@
                 merged[kv, first + i] = mean[:, i * HD : (i + 1) * HD]
 
             def head_of(z):
-                return z if slot == 0 else SIDE + z // 2
+                return z if slot == 0 else SIDE + z % 2
 
             for step in STEPS:
                 links.go(
@@ -275,7 +282,9 @@
 
         return [merge, row, near, far, close]
 
-    run_rounds([stage(kv, slot) for kv, slot in GATHER_PARTS], 1)
+    stages = [stage(kv, slot) for kv, slot in GATHER_PARTS]
+    for part, step in GATHER_ORDER:
+        stages[part][step]()
     for which, dst in enumerate((query_out, upstream_out)):
         for step in STEPS:
             links.got(("q", which, step), dst.at[shift(place.z, -step)])
@@ -301,7 +310,7 @@
 
     def unit_step(unit, carry):
         slot = unit // SIDE
-        unit_z = jnp.where(unit < SIDE, unit, jnp.where(unit == SIDE, place.z, SIDE - 1 - place.z))
+        unit_z = jnp.where(unit < SIDE, unit, jnp.where(unit == SIDE, place.z, place.partner_z()))
         frame = (place.y * SIDE + unit_z) * CORES + place.core
         count = live[frame]
         rows_live = count * KB
@@ -377,13 +386,13 @@
 
 
 SCATTER_SEMS = len(SCATTER_PARTS) * 14 + 2 * 4
-SCATTER_LOCAL = len(SCATTER_PARTS) + 4
+SCATTER_LOCAL = len(SCATTER_PARTS) + 5
 
 
 def scatter_kernel(
     key_part, value_part, att_in, dq_in, assign,
     attended, query_grad, grad_keys, grad_values,
-    twin, halves, fulls, outgoing, column, pieces, tokens, send, recv, local,
+    twin, halves, fulls, outgoing, column, pieces, tokens, assign_own, send, recv, local,
 ):
     place = Place()
     meet(place)
@@ -402,7 +411,7 @@
 
     for kv, slot in SCATTER_PARTS:
         send_twin(kv, slot)
-    mine = place.z // 2
+    mine = place.z % 2
     for which, (src, dst) in enumerate(((att_in, attended), (dq_in, query_grad))):
         for step in STEPS:
             links.go(
@@ -415,7 +424,8 @@
         )
         own.append(links.here(("q", which, 0), src.at[place.z], dst.at[:, cols(place.z)]))
         own.append(links.here(("q", which, 1), src.at[SIDE], dst.at[:, cols(SIDE + mine)]))
-    hot = slot_hot_of(assign)
+    links.here("assign", assign, assign_own).wait()
+    hot = slot_hot_of(assign_own)
     divisor = jnp.maximum(jnp.sum(hot, axis=1, keepdims=True), 1.0)
     hot = hot.astype(BF)
 
@@ -478,7 +488,7 @@
                 links.got(("z", kv, slot, step), pieces.at[kv, slot, shift(place.z, -step)])
             ready = [pieces[kv, slot, z].astype(F32) for z in range(SIDE)]
             if slot == 1:
-                ready = [ready[0] + ready[1], ready[2] + ready[3]]
+                ready = [ready[0] + ready[2], ready[1] + ready[3]]
             mean = jnp.concatenate([(one / divisor).astype(BF) for one in ready], axis=1)
             tokens[kv, :, first * HD : (first + count) * HD] = lax.dot_general(
                 hot, mean, (((0,), (0,)), ((), ())), preferred_element_type=F32
@@ -501,7 +511,9 @@
 
         return [start, relay, row, expand]
 
-    run_rounds([stage(kv, slot) for kv, slot in SCATTER_PARTS], 1)
+    stages = [stage(kv, slot) for kv, slot in SCATTER_PARTS]
+    for part, step in SCATTER_ORDER:
+        stages[part][step]()
 
     for which, dst in enumerate((attended, query_grad)):
         for step in STEPS:
@@ -519,6 +531,15 @@
     links.finish()
 
 
+def store_kernel(*refs):
+    sems = refs[-1]
+    copies = [pltpu.make_async_copy(refs[i], refs[4 + i], sems.at[i]) for i in range(4)]
+    for copy in copies:
+        copy.start()
+    for copy in copies:
+        copy.wait()
+
+
 ANY = pl.BlockSpec(memory_space=pl.ANY)
 HBM = pl.BlockSpec(memory_space=pltpu.HBM)
 VMEM = pl.BlockSpec(memory_space=pltpu.VMEM)
@@ -527,7 +548,10 @@
 
 
 def body(queries, keys_in, values_in, grad_out, assign, pattern, live_blocks):
-    assign_rows = assign.reshape(1, TOK)
+    keys_in, values_in, queries, grad_out, assign_rows = (
+        pltpu.with_memory_space_constraint(one, pltpu.HBM)
+        for one in (keys_in, values_in, queries, grad_out, assign.reshape(1, TOK))
+    )
     shape = jax.ShapeDtypeStruct
     dma = pltpu.SemaphoreType.DMA
     spread = (2, SIDE, CORES, SIDE, SLOTS, HD)
@@ -539,11 +563,12 @@
             shape((UNITS, TOK, HD), BF),
             shape((UNITS, TOK, HD), BF),
         ),
-        in_specs=[HBM, HBM, HBM, HBM, VMEM],
+        in_specs=[HBM, HBM, HBM, HBM, HBM],
         out_specs=(VMEM, VMEM, VMEM, VMEM),
         scratch_shapes=[
             pltpu.VMEM((2, TOK, WIDTH), BF),
             pltpu.VMEM((2, HEADS_X, SLOTS, HD), BF),
+            pltpu.VMEM((1, TOK), jnp.int32),
             dma((GATHER_SEMS,)),
             dma((GATHER_SEMS,)),
             dma((GATHER_LOCAL,)),
@@ -581,7 +606,7 @@
         query_units, upstream_units,
     )
 
-    return pl.pallas_call(
+    results = pl.pallas_call(
         scatter_kernel,
         out_shape=(
             shape(queries.shape, BF),
@@ -589,7 +614,7 @@
             shape(keys_in.shape, BF),
             shape(keys_in.shape, BF),
         ),
-        in_specs=[VMEM, VMEM, VMEM, VMEM, VMEM],
+        in_specs=[VMEM, VMEM, VMEM, VMEM, HBM],
         out_specs=(ANY, ANY, ANY, ANY),
         scratch_shapes=[
             pltpu.VMEM((2, 2, SIDE, SIDE, SLOTS, HD), BF),
@@ -599,6 +624,7 @@
             pltpu.VMEM((2, 2, SIDE, SLOTS, HD), BF),
             pltpu.VMEM((2, 2, SIDE, SLOTS, HD), BF),
             pltpu.VMEM((2, TOK, WIDTH), BF),
+            pltpu.VMEM((1, TOK), jnp.int32),
             dma((SCATTER_SEMS,)),
             dma((SCATTER_SEMS,)),
             dma((SCATTER_LOCAL,)),
@@ -608,6 +634,14 @@
         ),
         name="scatter",
     )(key_part.reshape(spread), value_part.reshape(spread), att_units, dq_units, assign_rows)
+    return pl.pallas_call(
+        store_kernel,
+        out_shape=tuple(shape(one.shape, BF) for one in results),
+        in_specs=[ANY] * 4,
+        out_specs=(HBM,) * 4,
+        scratch_shapes=[dma((4,))],
+        name="store",
+    )(*results)
 
 
 def solution(mesh):

time: 115 us -> 204 us (1.77)
  Pallas kernels: 105 us -> 200 us
  local copies, waits for them, and re-layouts: 8.74 us -> 3.55 us
    pallas_call x0 -> x1, Pallas kernels: none -> 96.4 us  [body(): pl.pallas_call(store_kernel, out_shape=tuple((shape(one.shape, BF) for on...]
    unnamed x18 -> x12, local copies, waits for them, and re-layouts: 8.74 us -> 3.55 us
    pallas_call x1, Pallas kernels: 50.1 us -> 47 us  [body(): pl.pallas_call(gather_kernel, out_shape=(shape(spread, BF), shape(spread,...]
where the time goes in v2:
time: 204 us
  Pallas kernels  200 us (98%)
  local copies, waits for them, and re-layouts  3.55 us (2%)
    pallas_call x1, Pallas kernels, body(): pl.pallas_call(store_kernel, out_shape=tuple((shape(one.shape, BF) for on...  96.4 us
    pallas_call x1, Pallas kernels, body(): pl.pallas_call(gather_kernel, out_shape=(shape(spread, BF), shape(spread,...  47 us
    pallas_call x1, Pallas kernels, body(): pl.pallas_call(scatter_kernel, out_shape=(shape(queries.shape, BF), shape...  43.8 us
    pallas_call x1, Pallas kernels, body(): pl.pallas_call(attention_kernel, out_shape=(shape((UNITS, TOK, HD), BF),...  12.5 us

profile of v2, /device:TPU:0, one launch (start us, length us, event | category | flops | bytes accessed | tf_op | source)
XLA Modules:
  0.0 203.9 jit_solution(7296122671941071341)
XLA Ops:
  0.6 0.0 copy-start.5
  0.6 0.0 copy-start.4
  0.7 47.0 %gather.1 = (bf16[2,4,2,4,128,128]{5,4,3,2,1,0:T(8,128)(2,1)S(1)}, bf16[2,4,2,4,128,128]{5,4,3,2,1,0:T(8,128)(2,1)S(1)}, bf16[6,512,128]{2,1,0:T(8,128)(2,1)S(1)}, bf16[6,512,128]{2,1,0:T(8,128)(2,1)S(1)}) custom-call(bf16[128,3072]{1,0:T(8,128)(2,1)} %keys.1, bf16[128,3072]{1,0:T(8,128)(2,1)} %values.1, bf16[512,768]{1,0:T(8,128)(2,1)} %queries.1, ...), custom_call_target="tpu_custom_call" | custom-call | tf_op jit(solution)/shard_map/gather/pallas_call | solution.py:558
  47.6 0.0 copy-done.5
  47.6 0.0 copy-done.4
  47.6 12.5 %attention.1 = (bf16[6,512,128]{2,1,0:T(8,128)(2,1)S(1)}, bf16[6,512,128]{2,1,0:T(8,128)(2,1)S(1)}, bf16[2,64,64,128]{3,2,1,0:T(8,128)(2,1)S(1)}, bf16[2,64,64,128]{3,2,1,0:T(8,128)(2,1)S(1)}) custom-call(s32[16,32]{1,0:T(8,128)S(1)} %bitcast.10, s32[32]{0:T(128)S(1)} %copy-done.5, bf16[2,64,64,128]{3,2,1,0:T(8,128)(2,1)S(1)} %bitcast.8, ...), custom_call_target="tpu_custom_call" | custom-call | tf_op jit(solution)/shard_map/attention/pallas_call | solution.py:584
  60.1 43.8 %scatter.1 = (bf16[512,768]{1,0:T(8,128)(2,1)S(1)}, bf16[512,768]{1,0:T(8,128)(2,1)S(1)}, bf16[128,3072]{1,0:T(8,128)(2,1)S(1)}, bf16[128,3072]{1,0:T(8,128)(2,1)S(1)}) custom-call(bf16[2,4,2,4,128,128]{5,4,3,2,1,0:T(8,128)(2,1)S(1)} %bitcast.6, bf16[2,4,2,4,128,128]{5,4,3,2,1,0:T(8,128)(2,1)S(1)} %bitcast.7, ...), custom_call_target="tpu_custom_call" | custom-call | tf_op jit(solution)/shard_map/scatter/pallas_call | solution.py:609
  103.9 0.0 copy-start
  103.9 0.9 copy-done
  104.8 0.0 copy-start.1
  104.8 0.9 copy-done.1
  105.7 0.0 copy-start.2
  105.7 0.9 copy-done.2
  106.6 0.0 copy-start.3
  106.6 0.9 copy-done.3
  107.5 96.4 %store.1 = (bf16[512,768]{1,0:T(8,128)(2,1)}, bf16[512,768]{1,0:T(8,128)(2,1)}, bf16[128,3072]{1,0:T(8,128)(2,1)}, bf16[128,3072]{1,0:T(8,128)(2,1)}) custom-call(bf16[512,768]{1,0:T(8,128)(2,1)} %copy-done, bf16[512,768]{1,0:T(8,128)(2,1)} %copy-done.1, bf16[128,3072]{1,0:T(8,128)(2,1)} %copy-done.2, bf16[128,3072]{1,0:T(8,128)(2,1)} %copy-done.3), custom_call_target="tpu_custom_call" | custom-call | tf_op jit(solution)/shard_map/store/pallas_call | solution.py:637
Async XLA Ops:
  0.6 47.0 %copy-start.5 = (s32[32]{0:T(128)S(1)}, s32[32]{0:T(128)}, u32[]{:S(2)}) copy-start(s32[32]{0:T(128)} %live.1) | copy-start | bytes 388
  0.6 47.0 %copy-start.4 = (s32[32,16]{0,1:T(8,128)S(1)}, s32[32,16]{0,1:T(8,128)}, u32[]{:S(2)}) copy-start(s32[32,16]{0,1:T(8,128)} %param.12) | copy-start | bytes 6148
  103.9 0.9 copy-start
  104.8 0.9 copy-start.1
  105.7 0.9 copy-start.2
  106.6 0.9 copy-start.3

commit v3 on v2

--- a/solution.py
+++ b/solution.py
@@ -637,9 +637,10 @@
     return pl.pallas_call(
         store_kernel,
         out_shape=tuple(shape(one.shape, BF) for one in results),
-        in_specs=[ANY] * 4,
+        in_specs=[VMEM] * 4,
         out_specs=(HBM,) * 4,
         scratch_shapes=[dma((4,))],
+        compiler_params=pltpu.CompilerParams(vmem_limit_bytes=VMEM_LIMIT),
         name="store",
     )(*results)
 

time: 204 us -> 106 us (0.52)
  Pallas kernels: 200 us -> 106 us
  local copies, waits for them, and re-layouts: 3.55 us -> 0.01 us
    pallas_call x1, Pallas kernels: 96.4 us -> 1.69 us  [body(): pl.pallas_call(store_kernel, out_shape=tuple((shape(one.shape, BF) for on...]
    unnamed x12 -> x4, local copies, waits for them, and re-layouts: 3.55 us -> 0.01 us
where the time goes in v3:
time: 106 us
  Pallas kernels  106 us (100%)
    pallas_call x1, Pallas kernels, body(): pl.pallas_call(gather_kernel, out_shape=(shape(spread, BF), shape(spread,...  47 us
    pallas_call x1, Pallas kernels, body(): pl.pallas_call(scatter_kernel, out_shape=(shape(queries.shape, BF), shape...  43.4 us
    pallas_call x1, Pallas kernels, body(): pl.pallas_call(attention_kernel, out_shape=(shape((UNITS, TOK, HD), BF),...  13.5 us

profile of v3, /device:TPU:0, one launch (start us, length us, event | category | flops | bytes accessed | tf_op | source)
XLA Modules:
  0.0 106.3 jit_solution(7589820905679155560)
XLA Ops:
  0.6 0.0 copy-start.1
  0.6 0.0 copy-start
  0.7 47.0 %gather.1 = (bf16[2,4,2,4,128,128]{5,4,3,2,1,0:T(8,128)(2,1)S(1)}, bf16[2,4,2,4,128,128]{5,4,3,2,1,0:T(8,128)(2,1)S(1)}, bf16[6,512,128]{2,1,0:T(8,128)(2,1)S(1)}, bf16[6,512,128]{2,1,0:T(8,128)(2,1)S(1)}) custom-call(bf16[128,3072]{1,0:T(8,128)(2,1)} %keys.1, bf16[128,3072]{1,0:T(8,128)(2,1)} %values.1, bf16[512,768]{1,0:T(8,128)(2,1)} %queries.1, ...), custom_call_target="tpu_custom_call" | custom-call | tf_op jit(solution)/shard_map/gather/pallas_call | solution.py:558
  47.6 0.0 copy-done.1
  47.6 0.0 copy-done
  47.6 13.5 %attention.1 = (bf16[6,512,128]{2,1,0:T(8,128)(2,1)S(1)}, bf16[6,512,128]{2,1,0:T(8,128)(2,1)S(1)}, bf16[2,64,64,128]{3,2,1,0:T(8,128)(2,1)S(1)}, bf16[2,64,64,128]{3,2,1,0:T(8,128)(2,1)S(1)}) custom-call(s32[16,32]{1,0:T(8,128)S(1)} %bitcast.10, s32[32]{0:T(128)S(1)} %copy-done.1, bf16[2,64,64,128]{3,2,1,0:T(8,128)(2,1)S(1)} %bitcast.8, ...), custom_call_target="tpu_custom_call" | custom-call | tf_op jit(solution)/shard_map/attention/pallas_call | solution.py:584
  61.2 43.4 %scatter.1 = (bf16[512,768]{1,0:T(8,128)(2,1)S(1)}, bf16[512,768]{1,0:T(8,128)(2,1)S(1)}, bf16[128,3072]{1,0:T(8,128)(2,1)S(1)}, bf16[128,3072]{1,0:T(8,128)(2,1)S(1)}) custom-call(bf16[2,4,2,4,128,128]{5,4,3,2,1,0:T(8,128)(2,1)S(1)} %bitcast.6, bf16[2,4,2,4,128,128]{5,4,3,2,1,0:T(8,128)(2,1)S(1)} %bitcast.7, ...), custom_call_target="tpu_custom_call" | custom-call | tf_op jit(solution)/shard_map/scatter/pallas_call | solution.py:609
  104.6 1.7 %store.1 = (bf16[512,768]{1,0:T(8,128)(2,1)}, bf16[512,768]{1,0:T(8,128)(2,1)}, bf16[128,3072]{1,0:T(8,128)(2,1)}, bf16[128,3072]{1,0:T(8,128)(2,1)}) custom-call(bf16[512,768]{1,0:T(8,128)(2,1)S(1)} %get-tuple-element.24.refs_0_, bf16[512,768]{1,0:T(8,128)(2,1)S(1)} %get-tuple-element.25.refs_1_, bf16[128,3072]{1,0:T(8,128)(2,1)S(1)} %get-tuple-element.26.refs_2_, ...), custom_call_target="tpu_custom_call" | custom-call | tf_op jit(solution)/shard_map/store/pallas_call | solution.py:637
Async XLA Ops:
  0.6 47.0 %copy-start.1 = (s32[32]{0:T(128)S(1)}, s32[32]{0:T(128)}, u32[]{:S(2)}) copy-start(s32[32]{0:T(128)} %live.1) | copy-start | bytes 388
  0.6 47.0 %copy-start = (s32[32,16]{0,1:T(8,128)S(1)}, s32[32,16]{0,1:T(8,128)}, u32[]{:S(2)}) copy-start(s32[32,16]{0,1:T(8,128)} %param.12) | copy-start | bytes 6148

commit v4 on v3

--- a/solution.py
+++ b/solution.py
@@ -243,7 +243,7 @@
                     place.ring("z", step),
                 )
             out[slot, place.y, place.core, place.z] = merged[kv, head_of(place.z)]
-            if (kv, slot) == GATHER_PARTS[0]:
+            if (kv, slot) == GATHER_PARTS[3]:
                 send_queries(1)
 
         def row():

time: 106 us -> 98.8 us (0.932)
  Pallas kernels: 106 us -> 97.9 us
    pallas_call x1, Pallas kernels: 47 us -> 41.9 us  [body(): pl.pallas_call(gather_kernel, out_shape=(shape(spread, BF), shape(spread,...]
    pallas_call x1, Pallas kernels: 13.5 us -> 11.1 us  [body(): pl.pallas_call(attention_kernel, out_shape=(shape((UNITS, TOK, HD), BF),...]
where the time goes in v4:
time: 98.8 us; the launch traced here: 98.6 us
  Pallas kernels  97.9 us (99%)
    pallas_call x1, Pallas kernels, body(): pl.pallas_call(scatter_kernel, out_shape=(shape(queries.shape, BF), shape...  43.3 us
    pallas_call x1, Pallas kernels, body(): pl.pallas_call(gather_kernel, out_shape=(shape(spread, BF), shape(spread,...  41.9 us
    pallas_call x1, Pallas kernels, body(): pl.pallas_call(attention_kernel, out_shape=(shape((UNITS, TOK, HD), BF),...  11.1 us

profile of v4, /device:TPU:0, one launch (start us, length us, event | category | flops | bytes accessed | tf_op | source)
XLA Modules:
  0.0 98.6 jit_solution(834621993713698452)
XLA Ops:
  0.6 0.0 copy-start.1
  0.6 0.0 copy-start
  0.7 41.9 %gather.1 = (bf16[2,4,2,4,128,128]{5,4,3,2,1,0:T(8,128)(2,1)S(1)}, bf16[2,4,2,4,128,128]{5,4,3,2,1,0:T(8,128)(2,1)S(1)}, bf16[6,512,128]{2,1,0:T(8,128)(2,1)S(1)}, bf16[6,512,128]{2,1,0:T(8,128)(2,1)S(1)}) custom-call(bf16[128,3072]{1,0:T(8,128)(2,1)} %keys.1, bf16[128,3072]{1,0:T(8,128)(2,1)} %values.1, bf16[512,768]{1,0:T(8,128)(2,1)} %queries.1, ...), custom_call_target="tpu_custom_call" | custom-call | tf_op jit(solution)/shard_map/gather/pallas_call | solution.py:558
  42.5 0.0 copy-done.1
  42.5 0.0 copy-done
  42.5 11.1 %attention.1 = (bf16[6,512,128]{2,1,0:T(8,128)(2,1)S(1)}, bf16[6,512,128]{2,1,0:T(8,128)(2,1)S(1)}, bf16[2,64,64,128]{3,2,1,0:T(8,128)(2,1)S(1)}, bf16[2,64,64,128]{3,2,1,0:T(8,128)(2,1)S(1)}) custom-call(s32[16,32]{1,0:T(8,128)S(1)} %bitcast.10, s32[32]{0:T(128)S(1)} %copy-done.1, bf16[2,64,64,128]{3,2,1,0:T(8,128)(2,1)S(1)} %bitcast.8, ...), custom_call_target="tpu_custom_call" | custom-call | tf_op jit(solution)/shard_map/attention/pallas_call | solution.py:584
  53.6 43.3 %scatter.1 = (bf16[512,768]{1,0:T(8,128)(2,1)S(1)}, bf16[512,768]{1,0:T(8,128)(2,1)S(1)}, bf16[128,3072]{1,0:T(8,128)(2,1)S(1)}, bf16[128,3072]{1,0:T(8,128)(2,1)S(1)}) custom-call(bf16[2,4,2,4,128,128]{5,4,3,2,1,0:T(8,128)(2,1)S(1)} %bitcast.6, bf16[2,4,2,4,128,128]{5,4,3,2,1,0:T(8,128)(2,1)S(1)} %bitcast.7, ...), custom_call_target="tpu_custom_call" | custom-call | tf_op jit(solution)/shard_map/scatter/pallas_call | solution.py:609
  96.9 1.7 %store.1 = (bf16[512,768]{1,0:T(8,128)(2,1)}, bf16[512,768]{1,0:T(8,128)(2,1)}, bf16[128,3072]{1,0:T(8,128)(2,1)}, bf16[128,3072]{1,0:T(8,128)(2,1)}) custom-call(bf16[512,768]{1,0:T(8,128)(2,1)S(1)} %get-tuple-element.24.refs_0_, bf16[512,768]{1,0:T(8,128)(2,1)S(1)} %get-tuple-element.25.refs_1_, bf16[128,3072]{1,0:T(8,128)(2,1)S(1)} %get-tuple-element.26.refs_2_, ...), custom_call_target="tpu_custom_call" | custom-call | tf_op jit(solution)/shard_map/store/pallas_call | solution.py:637
Async XLA Ops:
  0.6 41.9 %copy-start.1 = (s32[32]{0:T(128)S(1)}, s32[32]{0:T(128)}, u32[]{:S(2)}) copy-start(s32[32]{0:T(128)} %live.1) | copy-start | bytes 388
  0.6 41.9 %copy-start = (s32[32,16]{0,1:T(8,128)S(1)}, s32[32,16]{0,1:T(8,128)}, u32[]{:S(2)}) copy-start(s32[32,16]{0,1:T(8,128)} %param.12) | copy-start | bytes 6148

commit v5 on v4

v5 whole, which is shorter than its diff:
```python
import math

import jax
import jax.numpy as jnp
from jax import lax
from jax.experimental import pallas as pl
from jax.experimental.pallas import tpu as pltpu
from jax.sharding import PartitionSpec as P

HD = 128
KB = 64
NSEL = 16
SIDE = 4
CORES = 2
HEADS_X = 6
WIDTH = HEADS_X * HD
TOK = 512
TOK_DEV = TOK // SIDE
SLOTS = 128
SLOT_UNITS = (4, 2)
CHUNK = 512
SCALE = 1.0 / math.sqrt(HD)
MESH = pl.DeviceIdType.MESH
BF = jnp.bfloat16
F32 = jnp.float32
VMEM_LIMIT = 44 * 1024 * 1024
STORE_LIMIT = 8 * 1024 * 1024
GROUP = SIDE * SLOTS // KB
LOG2_E = math.log2(math.e)
STEPS = (1, -1, 2)
GROUPS = ((0, SIDE), (SIDE, HEADS_X - SIDE))
GATHER_PARTS = ((0, 1), (1, 1), (0, 0), (1, 0))
GATHER_STRAIGHT = GATHER_PARTS[3:]
SCATTER_STRAIGHT = ((1, 0),)


class Place:
    def __init__(self):
        frame = lax.axis_index("frame")
        self.x = lax.axis_index("head")
        self.core = frame % CORES
        self.z = (frame // CORES) % SIDE
        self.y = frame // (CORES * SIDE)

    def device(self, y, z, core, x):
        return {"frame": (y * SIDE + z) * CORES + core, "head": x}

    def ring(self, axis, step):
        at = {"x": self.x, "y": self.y, "z": self.z}
        at[axis] = (at[axis] + step + SIDE) % SIDE
        return self.device(at["y"], at["z"], self.core, at["x"])

    def sibling(self):
        return self.device(self.y, self.z, 1 - self.core, self.x)

    def partner_z(self):
        return jnp.where(self.core == 0, self.z + 1 - 2 * (self.z % 2), SIDE - 1 - self.z)

    def partner(self):
        return self.device(self.y, self.partner_z(), self.core, self.x)


def shift(at, step):
    return (at + step + SIDE) % SIDE


def meet(place):
    partners = [place.sibling()]
    partners += [place.ring(axis, step) for axis in ("x", "y", "z") for step in STEPS]
    barrier = pltpu.get_barrier_semaphore()
    for target in partners:
        pl.semaphore_signal(barrier, inc=1, device_id=target, device_id_type=MESH)
    pl.semaphore_wait(barrier, len(partners))


class Links:
    def __init__(self, place, send, recv, local):
        self.send, self.recv, self.local = send, recv, local
        self.anyone = place.sibling()
        self.started = []
        self.names = {}
        self.local_names = {}

    def sem(self, name):
        return self.names.setdefault(name, len(self.names))

    def remote(self, name, src, dst, target):
        sem = self.sem(name)
        return pltpu.make_async_remote_copy(
            src_ref=src,
            dst_ref=dst,
            send_sem=self.send.at[sem],
            recv_sem=self.recv.at[sem],
            device_id=target,
            device_id_type=MESH,
        )

    def go(self, name, src, dst, target):
        copy = self.remote(name, src, dst, target)
        copy.start()
        self.started.append(copy)

    def got(self, name, region):
        self.remote(name, region, region, self.anyone).wait_recv()

    def here(self, name, src, dst):
        sem = self.local_names.setdefault(name, len(self.local_names))
        copy = pltpu.make_async_copy(src, dst, self.local.at[sem])
        copy.start()
        return copy

    def finish(self):
        for copy in self.started:
            copy.wait_send()


def low(ref):
    return ref.at[pl.ds(0, GROUP // 2)]


def high(ref):
    return ref.at[pl.ds(GROUP // 2, GROUP // 2)]


def spot_of(block):
    owner = block // 2
    y, z, core = owner // (CORES * SIDE), (owner // CORES) % SIDE, owner % CORES
    return ((y * CORES + core) * SIDE + z) * 2 + block % 2


def cols(head, count=1):
    return pl.ds(pl.multiple_of(head * HD, HD), count * HD)


def token_rows(x):
    return pl.ds(pl.multiple_of(x * TOK_DEV, TOK_DEV), TOK_DEV)


def slot_hot_of(assign):
    slots = lax.broadcasted_iota(jnp.int32, (SLOTS, TOK), 0)
    return (slots == assign[0:1, :]).astype(F32)


SEMS = 4 * 14 + 2 * 4 + 4 * 14 + 2 * 4
LOCAL = 4 + 4 + 1 + 4 + 4
ALL_FRAMES = SIDE * SIDE * CORES
ALL_SPOTS = ALL_FRAMES * SLOTS // KB
DEAD = NSEL
ENTRIES = NSEL + 1


def layer_kernel(
    keys, values, queries, upstream, assign, spots, entries, biases,
    attended, query_grad, grad_keys, grad_values,
    keys0, keys1, values0, values1, tokens, merged, assign_own, query_in, upstream_in,
    ksel, vsel, expo, prob_grad, key_part0, key_part1, value_part0, value_part1, att_out, dq_out, dense,
    twin, halves, fulls, outgoing, column, pieces, token_out, send, recv, local,
):
    place = Place()
    meet(place)
    links = Links(place, send, recv, local)
    sources = (keys, values)
    every = ((keys0, keys1), (values0, values1))
    parts = ((key_part0, key_part1), (value_part0, value_part1))
    outs = (grad_keys, grad_values)
    own = {}
    mine = place.z % 2

    def send_tokens(kv, slot):
        first, count = GROUPS[slot]
        for step in STEPS:
            links.go(
                ("x", kv, slot, step),
                sources[kv].at[:, cols(shift(place.x, step) * HEADS_X + first, count)],
                tokens.at[kv, token_rows(place.x), cols(first, count)],
                place.ring("x", step),
            )
        own[kv, slot] = links.here(
            ("x", kv, slot),
            sources[kv].at[:, cols(place.x * HEADS_X + first, count)],
            tokens.at[kv, token_rows(place.x), cols(first, count)],
        )

    moved = ((queries, query_in), (upstream, upstream_in))

    def send_rows(which):
        src, dst = moved[which]
        for step in STEPS:
            links.go(
                ("q", which, step), src.at[:, cols(shift(place.z, step))], dst.at[place.z],
                place.ring("z", step),
            )
        own["q", which, 0] = links.here(("q", which, 0), src.at[:, cols(place.z)], dst.at[place.z])

    def send_pair(which):
        src, dst = moved[which]
        links.go(
            ("q", which, "partner"), src.at[:, cols(SIDE + 1 - mine)], dst.at[SIDE + 1],
            place.partner(),
        )
        own["q", which, 1] = links.here(
            ("q", which, 1), src.at[:, cols(SIDE + mine)], dst.at[SIDE]
        )

    def rows_arrived():
        for which, (_, dst) in enumerate(moved):
            for step in STEPS:
                links.got(("q", which, step), dst.at[shift(place.z, -step)])
            own["q", which, 0].wait()

    def pair_arrived():
        for which, (_, dst) in enumerate(moved):
            links.got(("q", which, "partner"), dst.at[SIDE + 1])
            own["q", which, 1].wait()

    send_tokens(*GATHER_PARTS[0])
    send_tokens(*GATHER_PARTS[1])
    send_pair(0)
    send_pair(1)
    send_rows(0)
    send_tokens(*GATHER_PARTS[2])
    send_tokens(*GATHER_PARTS[3])
    links.here("assign", assign, assign_own).wait()
    hot = slot_hot_of(assign_own)
    divisor = jnp.maximum(jnp.sum(hot, axis=1, keepdims=True), 1.0)
    hot = hot.astype(BF)
    for kv in range(2):
        for slot, count in enumerate(SLOT_UNITS):
            for at in range(count):
                parts[kv][slot][at * ENTRIES + DEAD] = jnp.zeros((KB, HD), BF)

    def group(y, core):
        return pl.ds((y * CORES + core) * GROUP, GROUP)

    def gather_stage(kv, slot):
        first, count = GROUPS[slot]
        out = every[kv][slot]
        straight = (kv, slot) in GATHER_STRAIGHT

        def region(step):
            return out.at[group(shift(place.y, step), place.core)]

        def cell(z):
            return pl.ds((place.y * CORES + place.core) * GROUP + z * 2, 2)

        def pass_on(step):
            links.go(("s", kv, slot, step), region(step), region(step), place.sibling())

        def merge():
            own[kv, slot].wait()
            for step in STEPS:
                links.got(
                    ("x", kv, slot, step),
                    tokens.at[kv, token_rows(shift(place.x, -step)), cols(first, count)],
                )
            sums = jnp.dot(
                hot, tokens[kv, :, first * HD : (first + count) * HD], preferred_element_type=F32
            )
            mean = (sums / divisor).astype(BF)
            for i in range(count):
                merged[kv, first + i] = mean[:, i * HD : (i + 1) * HD].reshape(2, KB, HD)

            def head_of(z):
                return z if slot == 0 else SIDE + z % 2

            for step in STEPS:
                links.go(
                    ("z", kv, slot, step),
                    merged.at[kv, head_of(shift(place.z, step))],
                    out.at[cell(place.z)],
                    place.ring("z", step),
                )
            out[cell(place.z)] = merged[kv, head_of(place.z)]
            if (kv, slot) == GATHER_PARTS[3]:
                send_rows(1)

        def row():
            for step in STEPS:
                links.got(("z", kv, slot, step), out.at[cell(shift(place.z, -step))])
            for step in STEPS if straight else STEPS[:2]:
                links.go(("y", kv, slot, step), region(0), region(0), place.ring("y", step))
            pass_on(0)

        def near():
            links.got(("y", kv, slot, 1), region(-1))
            if not straight:
                links.go(("f", kv, slot, 1), low(region(-1)), low(region(-1)), place.ring("y", 1))
            pass_on(-1)
            links.got(("y", kv, slot, -1), region(1))
            if not straight:
                links.go(("f", kv, slot, -1), high(region(1)), high(region(1)), place.ring("y", -1))
            pass_on(1)

        def far():
            if straight:
                links.got(("y", kv, slot, 2), region(2))
            else:
                links.got(("f", kv, slot, 1), low(region(2)))
                links.got(("f", kv, slot, -1), high(region(2)))
            pass_on(2)

        def close():
            for step in (0, -1, 1, 2):
                links.got(
                    ("s", kv, slot, step),
                    out.at[group(shift(place.y, step), 1 - place.core)],
                )

        return merge, row, near, far, close

    def attend(slot, unit):
        every_key, every_value = every[0][slot], every[1][slot]
        at = unit - slot * SIDE
        rows = NSEL * KB
        for j in range(NSEL):
            spot = spots[unit * NSEL + j]
            ksel[j * KB : (j + 1) * KB, :] = every_key[spot]
            vsel[j * KB : (j + 1) * KB, :] = every_value[spot]
        q, g = query_in[unit], upstream_in[unit]
        q_t, g_t = q.T, g.T
        spans = [(a, a + CHUNK) for a in range(0, rows, CHUNK)]
        top = jnp.full((1, TOK), -jnp.inf, F32)
        for a, b in spans:
            scores = jnp.dot(ksel[a:b, :], q_t, preferred_element_type=F32)
            for c in range(a, b, KB):
                block = scores[c - a : c - a + KB] + biases[unit * NSEL + c // KB]
                expo[c : c + KB, :] = block
                top = jnp.maximum(top, jnp.max(block, axis=0, keepdims=True))
            prob_grad[a:b, :] = jnp.dot(vsel[a:b, :], g_t, preferred_element_type=F32)
        top = top * (SCALE * LOG2_E)
        total = jnp.zeros((1, TOK), F32)
        weighted = jnp.zeros((HD, TOK), F32)
        for a, b in spans:
            weights = jnp.exp2(expo[a:b, :] * (SCALE * LOG2_E) - top)
            expo[a:b, :] = weights
            total = total + jnp.sum(weights, axis=0, keepdims=True)
            weighted = weighted + lax.dot_general(
                vsel[a:b, :], weights.astype(BF), (((0,), (0,)), ((), ())),
                preferred_element_type=F32,
            )
        inverse = 1.0 / total
        att_t = (weighted * inverse).astype(BF)
        att_out[unit] = att_t.T
        delta = jnp.sum(g_t.astype(F32) * att_t.astype(F32), axis=0, keepdims=True)
        dq = jnp.zeros((HD, TOK), F32)
        blocks = CHUNK // KB
        for a, b in spans:
            probs = expo[a:b, :] * inverse
            score_grad = (probs * (prob_grad[a:b, :] - delta)).astype(BF)
            dk = jnp.dot(score_grad, q, preferred_element_type=F32) * SCALE
            dv = jnp.dot(probs.astype(BF), g, preferred_element_type=F32)
            for kv, grads in enumerate((dk, dv)):
                into = pl.ds(at * ENTRIES + a // KB, blocks)
                parts[kv][slot][into] = grads.astype(BF).reshape(blocks, KB, HD)
            dq = dq + lax.dot_general(
                ksel[a:b, :], score_grad, (((0,), (0,)), ((), ())), preferred_element_type=F32
            )
        dq_out[unit] = (dq * SCALE).astype(BF).T

    results = ((att_out, attended), (dq_out, query_grad))

    def send_result(unit, step):
        for which, (src, dst) in enumerate(results):
            if step:
                links.go(
                    ("r", which, step), src.at[unit], dst.at[:, cols(place.z)], place.ring("z", step)
                )
            else:
                own["r", which, 0] = links.here(
                    ("r", which, 0), src.at[unit], dst.at[:, cols(place.z)]
                )

    def send_pair_result():
        for which, (src, dst) in enumerate(results):
            links.go(
                ("r", which, "partner"), src.at[SIDE + 1], dst.at[:, cols(SIDE + mine)],
                place.partner(),
            )
            own["r", which, 1] = links.here(
                ("r", which, 1), src.at[SIDE], dst.at[:, cols(SIDE + mine)]
            )

    def spread(kv, slot):
        def region(y, core):
            def one(i, carry):
                spot = (y * CORES + core) * GROUP + i
                total = jnp.zeros((KB, HD), F32)
                for at in range(SLOT_UNITS[slot]):
                    entry = entries[(slot * SIDE + at) * ALL_SPOTS + spot]
                    total = total + parts[kv][slot][entry].astype(F32)
                dense[kv, slot, spot] = total.astype(BF)
                return carry

            lax.fori_loop(0, GROUP, one, 0)

        for step in (2, 1, -1, 0):
            y = shift(place.y, step)
            region(y, 1 - place.core)
            links.go(
                ("t", kv, slot, step), dense.at[kv, slot, group(y, 1 - place.core)],
                twin.at[kv, slot, y], place.sibling(),
            )
        for step in (2, 1, -1, 0):
            region(shift(place.y, step), place.core)

    def scatter_stage(kv, slot):
        first, count = GROUPS[slot]
        straight = (kv, slot) in SCATTER_STRAIGHT
        half_in, full_in, out = halves.at[kv, slot], fulls.at[kv, slot], outgoing.at[kv, slot]

        def term(step):
            y = shift(place.y, step)
            links.got(("t", kv, slot, step), twin.at[kv, slot, y])
            here = dense[kv, slot, group(y, place.core)]
            return here.astype(F32) + twin[kv, slot, y].astype(F32)

        def start():
            out[2] = term(2).astype(BF)
            if straight:
                links.go(("w", kv, slot, 2), out.at[2], full_in.at[2], place.ring("y", 2))
                return
            links.go(("h", kv, slot, 1), low(out.at[2]), half_in.at[0], place.ring("y", 1))
            links.go(("h", kv, slot, -1), high(out.at[2]), half_in.at[1], place.ring("y", -1))

        def relay():
            ahead = term(1)
            behind = term(-1)
            half = GROUP // 2
            if straight:
                for at, step, value in ((0, 1, ahead), (1, -1, behind)):
                    out[at] = value.astype(BF)
                    links.go(
                        ("w", kv, slot, step), out.at[at], full_in.at[at], place.ring("y", step)
                    )
                return
            links.got(("h", kv, slot, 1), half_in.at[0])
            out[0, 0:half] = (ahead[0:half] + half_in[0].astype(F32)).astype(BF)
            out[0, half:GROUP] = ahead[half:GROUP].astype(BF)
            links.go(("w", kv, slot, 1), out.at[0], full_in.at[0], place.ring("y", 1))
            links.got(("h", kv, slot, -1), half_in.at[1])
            out[1, 0:half] = behind[0:half].astype(BF)
            out[1, half:GROUP] = (behind[half:GROUP] + half_in[1].astype(F32)).astype(BF)
            links.go(("w", kv, slot, -1), out.at[1], full_in.at[1], place.ring("y", -1))

        def total():
            value = term(0)
            links.got(("w", kv, slot, 1), full_in.at[0])
            links.got(("w", kv, slot, -1), full_in.at[1])
            value = value + full_in[0].astype(F32) + full_in[1].astype(F32)
            if straight:
                links.got(("w", kv, slot, 2), full_in.at[2])
                value = value + full_in[2].astype(F32)
            column[kv, slot] = value.astype(BF)
            for step in STEPS:
                links.go(
                    ("v", kv, slot, step),
                    column.at[kv, slot, pl.ds(shift(place.z, step) * 2, 2)],
                    pieces.at[kv, slot, place.z], place.ring("z", step),
                )
            pieces[kv, slot, place.z] = column[kv, slot, pl.ds(place.z * 2, 2)]

        def expand():
            for step in STEPS:
                links.got(("v", kv, slot, step), pieces.at[kv, slot, shift(place.z, -step)])
            ready = [pieces[kv, slot, z].astype(F32).reshape(SLOTS, HD) for z in range(SIDE)]
            if slot == 1:
                ready = [ready[0] + ready[2], ready[1] + ready[3]]
            mean = jnp.concatenate([(one / divisor).astype(BF) for one in ready], axis=1)
            token_out[kv, :, first * HD : (first + count) * HD] = lax.dot_general(
                hot, mean, (((0,), (0,)), ((), ())), preferred_element_type=F32
            ).astype(BF)
            to = cols(place.x * HEADS_X + first, count)
            for step in STEPS:
                links.go(
                    ("u", kv, slot, step),
                    token_out.at[kv, token_rows(shift(place.x, step)), cols(first, count)],
                    outs[kv].at[:, to],
                    place.ring("x", step),
                )
            own["u", kv, slot] = links.here(
                ("u", kv, slot),
                token_out.at[kv, token_rows(place.x), cols(first, count)],
                outs[kv].at[:, to],
            )

        return start, relay, total, expand

    (merge0, row0, near0, far0, close0), (merge1, row1, near1, far1, close1), (
        merge2, row2, near2, far2, close2,
    ), (merge3, row3, near3, far3, close3) = [gather_stage(kv, slot) for kv, slot in GATHER_PARTS]
    for step in (
        merge0, merge1, row0, row1, merge2, near0, near1, row2, far0, merge3, far1, row3, near2, far2,
        close0, close1, pair_arrived,
    ):
        step()

    def pair_step(i, carry):
        attend(1, SIDE + i)
        return carry

    lax.fori_loop(0, SLOT_UNITS[1], pair_step, 0)
    near3()
    far3()
    send_pair_result()
    spread(1, 1)
    spread(0, 1)
    close2()
    close3()
    rows_arrived()

    def ahead_step(i, carry):
        attend(0, shift(place.z, 1 + 2 * i))
        return carry

    def rest_step(i, carry):
        attend(0, shift(place.z, 2 + 2 * i))
        return carry

    value0, key0, value1, key1 = [
        scatter_stage(kv, slot) for kv, slot in ((1, 0), (0, 0), (1, 1), (0, 1))
    ]
    start, relay, total, expand = range(4)
    value1[start]()
    key1[start]()
    lax.fori_loop(0, 2, ahead_step, 0)
    send_result(shift(place.z, 1), 1)
    send_result(shift(place.z, -1), -1)
    value1[relay]()
    key1[relay]()
    lax.fori_loop(0, 2, rest_step, 0)
    send_result(shift(place.z, 2), 2)
    send_result(place.z, 0)
    value1[total]()
    key1[total]()
    spread(1, 0)
    value0[start]()
    value0[relay]()
    value1[expand]()
    key1[expand]()
    spread(0, 0)
    key0[start]()
    key0[relay]()
    value0[total]()
    value0[expand]()
    key0[total]()
    key0[expand]()

    for which, (_, dst) in enumerate(results):
        for step in STEPS:
            links.got(("r", which, step), dst.at[:, cols(shift(place.z, -step))])
        links.got(("r", which, "partner"), dst.at[:, cols(SIDE + 1 - mine)])
        own["r", which, 0].wait()
        own["r", which, 1].wait()
    for slot, (first, count) in enumerate(GROUPS):
        for kv in range(2):
            for step in STEPS:
                links.got(
                    ("u", kv, slot, step),
                    outs[kv].at[:, cols(shift(place.x, -step) * HEADS_X + first, count)],
                )
            own["u", kv, slot].wait()
    links.finish()


def prepare_kernel(pattern, live, spots, entries, biases):
    place = Place()
    for unit in range(sum(SLOT_UNITS)):
        z = unit if unit < SIDE else place.z if unit == SIDE else place.partner_z()
        frame = (place.y * SIDE + z) * CORES + place.core
        base = unit % SIDE * ENTRIES

        def clear(i, carry, unit=unit, base=base):
            entries[unit * ALL_SPOTS + i] = base + DEAD
            return carry

        lax.fori_loop(0, ALL_SPOTS, clear, 0, unroll=8)

        def note(j, carry, unit=unit, base=base, frame=frame):
            spot = spot_of(pattern[j, frame])
            alive = j < live[frame]
            spots[unit * NSEL + j] = spot
            biases[unit * NSEL + j] = jnp.where(alive, 0.0, -jnp.inf).astype(F32)
            entries[unit * ALL_SPOTS + spot] = jnp.where(alive, base + j, base + DEAD)
            return carry

        lax.fori_loop(0, NSEL, note, 0, unroll=4)


def store_kernel(*refs):
    sems = refs[-1]
    copies = [pltpu.make_async_copy(refs[i], refs[4 + i], sems.at[i]) for i in range(4)]
    for copy in copies:
        copy.start()
    for copy in copies:
        copy.wait()


ANY = pl.BlockSpec(memory_space=pl.ANY)
HBM = pl.BlockSpec(memory_space=pltpu.HBM)
VMEM = pl.BlockSpec(memory_space=pltpu.VMEM)
SMEM = pl.BlockSpec(memory_space=pltpu.SMEM)


def body(queries, keys_in, values_in, grad_out, assign, pattern, live_blocks):
    inputs = [
        pltpu.with_memory_space_constraint(one, pltpu.HBM)
        for one in (keys_in, values_in, queries, grad_out, assign.reshape(1, TOK))
    ]
    shape = jax.ShapeDtypeStruct
    dma = pltpu.SemaphoreType.DMA
    units = sum(SLOT_UNITS)
    lists = pl.pallas_call(
        prepare_kernel,
        out_shape=(
            shape((units * NSEL,), jnp.int32),
            shape((units * ALL_SPOTS,), jnp.int32),
            shape((units * NSEL,), F32),
        ),
        in_specs=[SMEM] * 2,
        out_specs=(SMEM,) * 3,
        compiler_params=pltpu.CompilerParams(vmem_limit_bytes=STORE_LIMIT),
        name="prepare",
    )(pattern.T, live_blocks)

    def half(*dims):
        return pltpu.VMEM(dims, BF)

    results = pl.pallas_call(
        layer_kernel,
        out_shape=(
            shape(queries.shape, BF),
            shape(queries.shape, BF),
            shape(keys_in.shape, BF),
            shape(keys_in.shape, BF),
        ),
        in_specs=[HBM] * 5 + [SMEM] * 3,
        out_specs=(ANY,) * 4,
        scratch_shapes=[
            half(ALL_SPOTS, KB, HD),
            half(ALL_SPOTS, KB, HD),
            half(ALL_SPOTS, KB, HD),
            half(ALL_SPOTS, KB, HD),
            half(2, TOK, WIDTH),
            half(2, HEADS_X, 2, KB, HD),
            pltpu.VMEM((1, TOK), jnp.int32),
            half(units, TOK, HD),
            half(units, TOK, HD),
            half(NSEL * KB, HD),
            half(NSEL * KB, HD),
            pltpu.VMEM((NSEL * KB, TOK), F32),
            pltpu.VMEM((NSEL * KB, TOK), F32),
            half(SLOT_UNITS[0] * ENTRIES, KB, HD),
            half(SLOT_UNITS[1] * ENTRIES, KB, HD),
            half(SLOT_UNITS[0] * ENTRIES, KB, HD),
            half(SLOT_UNITS[1] * ENTRIES, KB, HD),
            half(units, TOK, HD),
            half(units, TOK, HD),
            half(2, 2, ALL_SPOTS, KB, HD),
            half(2, 2, SIDE, GROUP, KB, HD),
            half(2, 2, 2, GROUP // 2, KB, HD),
            half(2, 2, 3, GROUP, KB, HD),
            half(2, 2, 3, GROUP, KB, HD),
            half(2, 2, GROUP, KB, HD),
            half(2, 2, SIDE, 2, KB, HD),
            half(2, TOK, WIDTH),
            dma((SEMS,)),
            dma((SEMS,)),
            dma((LOCAL,)),
        ],
        compiler_params=pltpu.CompilerParams(
            collective_id=0, has_side_effects=True, vmem_limit_bytes=VMEM_LIMIT
        ),
        name="layer",
    )(*inputs, *lists)
    return pl.pallas_call(
        store_kernel,
        out_shape=tuple(shape(one.shape, BF) for one in results),
        in_specs=[VMEM] * 4,
        out_specs=(HBM,) * 4,
        scratch_shapes=[dma((4,))],
        compiler_params=pltpu.CompilerParams(vmem_limit_bytes=STORE_LIMIT),
        name="store",
    )(*results)


def solution(mesh):
    return jax.shard_map(
        body,
        mesh=mesh,
        in_specs=(
            P("frame", "head"),
            P(("frame", "head"), None),
            P(("frame", "head"), None),
            P("frame", "head"),
            P("frame"),
            P(),
            P(),
        ),
        out_specs=(
            P("frame", "head"),
            P("frame", "head"),
            P(("frame", "head"), None),
            P(("frame", "head"), None),
        ),
        check_vma=False,
    )
```

time: 98.8 us -> 102 us (1.032)
  Pallas kernels: 97.9 us -> 100 us
  local copies, waits for them, and re-layouts: 0.01 us -> 1.34 us
    pallas_call x3 -> x2, Pallas kernels: 96.2 us -> 98.3 us  [the longest x1 94.4 us: body(): pl.pallas_call(layer_kernel, out_shape=(shape(queries.shape, BF), shape(q...]
    unnamed x4, local copies, waits for them, and re-layouts: 0.01 us -> 1.34 us
where the time goes in v5:
time: 102 us
  Pallas kernels  100 us (98%)
  local copies, waits for them, and re-layouts  1.34 us (1%)
    pallas_call x1, Pallas kernels, body(): pl.pallas_call(layer_kernel, out_shape=(shape(queries.shape, BF), shape(q...  94.4 us
    pallas_call x1, Pallas kernels, body(): pl.pallas_call(prepare_kernel, out_shape=(shape((units * NSEL,), jnp.int3...  3.92 us

profile of v5, /device:TPU:0, one launch (start us, length us, event | category | flops | bytes accessed | tf_op | source)
XLA Modules:
  0.0 102.0 jit_solution(2734433409682625797)
XLA Ops:
  0.6 0.0 copy-start.1
  0.6 0.6 copy-done.1
  1.3 0.0 copy-start
  1.3 0.7 copy-done
  2.0 3.9 %prepare.1 = (s32[96]{0:T(128)S(1)}, s32[384]{0:T(512)S(1)}, f32[96]{0:T(128)S(1)}) custom-call(s32[16,32]{1,0:T(8,128)S(1)} %bitcast.2, s32[32]{0:T(128)S(1)} %copy-done.1), custom_call_target="tpu_custom_call" | custom-call | tf_op jit(solution)/shard_map/prepare/pallas_call | solution.py:612
  5.9 94.4 %layer.1 = (bf16[512,768]{1,0:T(8,128)(2,1)S(1)}, bf16[512,768]{1,0:T(8,128)(2,1)S(1)}, bf16[128,3072]{1,0:T(8,128)(2,1)S(1)}, bf16[128,3072]{1,0:T(8,128)(2,1)S(1)}) custom-call(bf16[128,3072]{1,0:T(8,128)(2,1)} %keys.1, bf16[128,3072]{1,0:T(8,128)(2,1)} %values.1, bf16[512,768]{1,0:T(8,128)(2,1)} %queries.1, bf16[512,768]{1,0:T(8,128)(2,1)} %upstream.1, ...), custom_call_target="tpu_custom_call" | custom-call | tf_op jit(solution)/shard_map/layer/pallas_call | solution.py:628
  100.3 1.7 %store.1 = (bf16[512,768]{1,0:T(8,128)(2,1)}, bf16[512,768]{1,0:T(8,128)(2,1)}, bf16[128,3072]{1,0:T(8,128)(2,1)}, bf16[128,3072]{1,0:T(8,128)(2,1)}) custom-call(bf16[512,768]{1,0:T(8,128)(2,1)S(1)} %get-tuple-element.14.refs_0_, bf16[512,768]{1,0:T(8,128)(2,1)S(1)} %get-tuple-element.15.refs_1_, bf16[128,3072]{1,0:T(8,128)(2,1)S(1)} %get-tuple-element.16.refs_2_, ...), custom_call_target="tpu_custom_call" | custom-call | tf_op jit(solution)/shard_map/store/pallas_call | solution.py:675
Async XLA Ops:
  0.6 0.7 copy-start.1
  1.3 0.7 copy-start

commit v6 on v5

--- a/solution.py
+++ b/solution.py
@@ -23,15 +23,15 @@
 MESH = pl.DeviceIdType.MESH
 BF = jnp.bfloat16
 F32 = jnp.float32
-VMEM_LIMIT = 44 * 1024 * 1024
+VMEM_LIMIT = 50 * 1024 * 1024
 STORE_LIMIT = 8 * 1024 * 1024
 GROUP = SIDE * SLOTS // KB
 LOG2_E = math.log2(math.e)
 STEPS = (1, -1, 2)
 GROUPS = ((0, SIDE), (SIDE, HEADS_X - SIDE))
-GATHER_PARTS = ((0, 1), (1, 1), (0, 0), (1, 0))
-GATHER_STRAIGHT = GATHER_PARTS[3:]
-SCATTER_STRAIGHT = ((1, 0),)
+GATHER_PARTS = ((0, 1), (0, 0), (1, 0), (1, 1))
+GATHER_STRAIGHT = (GATHER_PARTS[0], GATHER_PARTS[3])
+SCATTER_STRAIGHT = ()
 
 
 class Place:
@@ -123,9 +123,8 @@
 
 
 def spot_of(block):
-    owner = block // 2
-    y, z, core = owner // (CORES * SIDE), (owner // CORES) % SIDE, owner % CORES
-    return ((y * CORES + core) * SIDE + z) * 2 + block % 2
+    y, z, core, half = block >> 4, (block >> 2) & 3, (block >> 1) & 1, block & 1
+    return (y << 4) + (core << 3) + (z << 1) + half
 
 
 def cols(head, count=1):
@@ -142,7 +141,7 @@
 
 
 SEMS = 4 * 14 + 2 * 4 + 4 * 14 + 2 * 4
-LOCAL = 4 + 4 + 1 + 4 + 4
+LOCAL = 4 + 4 + 4 + 4 + 4
 ALL_FRAMES = SIDE * SIDE * CORES
 ALL_SPOTS = ALL_FRAMES * SLOTS // KB
 DEAD = NSEL
@@ -150,15 +149,16 @@
 
 
 def layer_kernel(
-    keys, values, queries, upstream, assign, spots, entries, biases,
+    keys, values, queries, upstream, assign, pattern_in, live_in,
     attended, query_grad, grad_keys, grad_values,
     keys0, keys1, values0, values1, tokens, merged, assign_own, query_in, upstream_in,
-    ksel, vsel, expo, prob_grad, key_part0, key_part1, value_part0, value_part1, att_out, dq_out, dense,
-    twin, halves, fulls, outgoing, column, pieces, token_out, send, recv, local,
+    listed, expo, inverses, prob_grad, key_part0, key_part1, value_part0, value_part1, att_out, dq_out, dense,
+    twin, halves, fulls, outgoing, column, pieces, token_out, pattern, live, entries_out, entries, send, recv, local,
 ):
     place = Place()
+    links = Links(place, send, recv, local)
+    lists = [links.here("pattern", pattern_in, pattern), links.here("live", live_in, live)]
     meet(place)
-    links = Links(place, send, recv, local)
     sources = (keys, values)
     every = ((keys0, keys1), (values0, values1))
     parts = ((key_part0, key_part1), (value_part0, value_part1))
@@ -215,11 +215,11 @@
 
     send_tokens(*GATHER_PARTS[0])
     send_tokens(*GATHER_PARTS[1])
-    send_pair(0)
-    send_pair(1)
     send_rows(0)
     send_tokens(*GATHER_PARTS[2])
     send_tokens(*GATHER_PARTS[3])
+    for one in lists:
+        one.wait()
     links.here("assign", assign, assign_own).wait()
     hot = slot_hot_of(assign_own)
     divisor = jnp.maximum(jnp.sum(hot, axis=1, keepdims=True), 1.0)
@@ -271,7 +271,10 @@
                     place.ring("z", step),
                 )
             out[cell(place.z)] = merged[kv, head_of(place.z)]
-            if (kv, slot) == GATHER_PARTS[3]:
+            if (kv, slot) == GATHER_PARTS[0]:
+                send_pair(0)
+                send_pair(1)
+            if (kv, slot) == GATHER_PARTS[1]:
                 send_rows(1)
 
         def row():
@@ -308,52 +311,80 @@
 
         return merge, row, near, far, close
 
-    def attend(slot, unit):
-        every_key, every_value = every[0][slot], every[1][slot]
-        at = unit - slot * SIDE
-        rows = NSEL * KB
+    def frame_of(slot, at):
+        z = at if slot == 0 else jnp.where(at == 0, place.z, place.partner_z())
+        return (place.y * SIDE + z) * CORES + place.core
+
+    def note_entries():
+        lanes = lax.broadcasted_iota(jnp.int32, (1, HD), 1)
+        entries_out[...] = jnp.zeros_like(entries_out)
+        for slot, count in enumerate(SLOT_UNITS):
+            for at in range(count):
+                frame = frame_of(slot, at)
+                entry = jnp.full((1, HD), at * ENTRIES + DEAD, jnp.int32)
+                for j in range(NSEL):
+                    named = (lanes == spot_of(pattern[j, frame])) & (lanes * 0 + j < live[0, frame])
+                    entry = jnp.where(named, at * ENTRIES + j, entry)
+                entries_out[slot * SIDE + at : slot * SIDE + at + 1, :] = entry
+        links.here("entries", entries_out, entries).wait()
+
+    spans = [(a, a + CHUNK) for a in range(0, NSEL * KB, CHUNK)]
+    chunk_blocks = CHUNK // KB
+
+    def select(every_one, frame):
         for j in range(NSEL):
-            spot = spots[unit * NSEL + j]
-            ksel[j * KB : (j + 1) * KB, :] = every_key[spot]
-            vsel[j * KB : (j + 1) * KB, :] = every_value[spot]
-        q, g = query_in[unit], upstream_in[unit]
-        q_t, g_t = q.T, g.T
-        spans = [(a, a + CHUNK) for a in range(0, rows, CHUNK)]
+            listed[j * KB : (j + 1) * KB, :] = every_one[spot_of(pattern[j, frame])]
+
+    def keep(kv, slot, unit, a, grads):
+        into = pl.ds((unit - slot * SIDE) * ENTRIES + a // KB, chunk_blocks)
+        parts[kv][slot][into] = grads.astype(BF).reshape(chunk_blocks, KB, HD)
+
+    def weigh(slot, unit):
+        frame = frame_of(slot, unit - slot * SIDE)
+        select(every[0][slot], frame)
+        q_t, g = query_in[unit].T, upstream_in[unit]
         top = jnp.full((1, TOK), -jnp.inf, F32)
         for a, b in spans:
-            scores = jnp.dot(ksel[a:b, :], q_t, preferred_element_type=F32)
-            for c in range(a, b, KB):
-                block = scores[c - a : c - a + KB] + biases[unit * NSEL + c // KB]
-                expo[c : c + KB, :] = block
-                top = jnp.maximum(top, jnp.max(block, axis=0, keepdims=True))
-            prob_grad[a:b, :] = jnp.dot(vsel[a:b, :], g_t, preferred_element_type=F32)
+            scores = jnp.dot(listed[a:b, :], q_t, preferred_element_type=F32)
+            ids = lax.broadcasted_iota(jnp.int32, (CHUNK, TOK), 0) + a
+            scores = jnp.where(ids < live[0, frame] * KB, scores, -jnp.inf)
+            expo[unit, a:b, :] = scores
+            top = jnp.maximum(top, jnp.max(scores, axis=0, keepdims=True))
         top = top * (SCALE * LOG2_E)
         total = jnp.zeros((1, TOK), F32)
+        for a, b in spans:
+            weights = jnp.exp2(expo[unit, a:b, :] * (SCALE * LOG2_E) - top)
+            expo[unit, a:b, :] = weights
+            total = total + jnp.sum(weights, axis=0, keepdims=True)
+        inverse = 1.0 / total
+        inverses[unit] = inverse
+        for a, b in spans:
+            probs = (expo[unit, a:b, :] * inverse).astype(BF)
+            keep(1, slot, unit, a, jnp.dot(probs, g, preferred_element_type=F32))
+
+    def attend(slot, unit):
+        frame = frame_of(slot, unit - slot * SIDE)
+        select(every[1][slot], frame)
+        q, g_t = query_in[unit], upstream_in[unit].T
+        inverse = inverses[unit]
         weighted = jnp.zeros((HD, TOK), F32)
         for a, b in spans:
-            weights = jnp.exp2(expo[a:b, :] * (SCALE * LOG2_E) - top)
-            expo[a:b, :] = weights
-            total = total + jnp.sum(weights, axis=0, keepdims=True)
             weighted = weighted + lax.dot_general(
-                vsel[a:b, :], weights.astype(BF), (((0,), (0,)), ((), ())),
+                listed[a:b, :], expo[unit, a:b, :].astype(BF), (((0,), (0,)), ((), ())),
                 preferred_element_type=F32,
             )
-        inverse = 1.0 / total
+            prob_grad[a:b, :] = jnp.dot(listed[a:b, :], g_t, preferred_element_type=F32)
         att_t = (weighted * inverse).astype(BF)
         att_out[unit] = att_t.T
         delta = jnp.sum(g_t.astype(F32) * att_t.astype(F32), axis=0, keepdims=True)
+        select(every[0][slot], frame)
         dq = jnp.zeros((HD, TOK), F32)
-        blocks = CHUNK // KB
         for a, b in spans:
-            probs = expo[a:b, :] * inverse
+            probs = expo[unit, a:b, :] * inverse
             score_grad = (probs * (prob_grad[a:b, :] - delta)).astype(BF)
-            dk = jnp.dot(score_grad, q, preferred_element_type=F32) * SCALE
-            dv = jnp.dot(probs.astype(BF), g, preferred_element_type=F32)
-            for kv, grads in enumerate((dk, dv)):
-                into = pl.ds(at * ENTRIES + a // KB, blocks)
-                parts[kv][slot][into] = grads.astype(BF).reshape(blocks, KB, HD)
+            keep(0, slot, unit, a, jnp.dot(score_grad, q, preferred_element_type=F32) * SCALE)
             dq = dq + lax.dot_general(
-                ksel[a:b, :], score_grad, (((0,), (0,)), ((), ())), preferred_element_type=F32
+                listed[a:b, :], score_grad, (((0,), (0,)), ((), ())), preferred_element_type=F32
             )
         dq_out[unit] = (dq * SCALE).astype(BF).T
 
@@ -386,7 +417,7 @@
                 spot = (y * CORES + core) * GROUP + i
                 total = jnp.zeros((KB, HD), F32)
                 for at in range(SLOT_UNITS[slot]):
-                    entry = entries[(slot * SIDE + at) * ALL_SPOTS + spot]
+                    entry = entries[slot * SIDE + at, spot]
                     total = total + parts[kv][slot][entry].astype(F32)
                 dense[kv, slot, spot] = total.astype(BF)
                 return carry
@@ -485,65 +516,74 @@
 
         return start, relay, total, expand
 
-    (merge0, row0, near0, far0, close0), (merge1, row1, near1, far1, close1), (
-        merge2, row2, near2, far2, close2,
-    ), (merge3, row3, near3, far3, close3) = [gather_stage(kv, slot) for kv, slot in GATHER_PARTS]
-    for step in (
-        merge0, merge1, row0, row1, merge2, near0, near1, row2, far0, merge3, far1, row3, near2, far2,
-        close0, close1, pair_arrived,
-    ):
-        step()
-
-    def pair_step(i, carry):
-        attend(1, SIDE + i)
-        return carry
-
-    lax.fori_loop(0, SLOT_UNITS[1], pair_step, 0)
-    near3()
-    far3()
-    send_pair_result()
+    def work(what, slot, first, count):
+        def one(i, carry):
+            what(slot, SIDE + first + i if slot else shift(place.z, first + 2 * i))
+            return carry
+
+        lax.fori_loop(0, count, one, 0)
+
+    merge, row, near, far, close = range(5)
+    key1, key0, value0, value1 = [gather_stage(kv, slot) for kv, slot in GATHER_PARTS]
+    start, relay, total, expand = range(4)
+    key_grad1, key_grad0, value_grad0, value_grad1 = [
+        scatter_stage(kv, slot) for kv, slot in GATHER_PARTS
+    ]
+    note_entries()
+    key1[merge]()
+    key1[row]()
+    key0[merge]()
+    key1[near]()
+    key0[row]()
+    key1[far]()
+    value0[merge]()
+    key1[close]()
+    pair_arrived()
+    work(weigh, 1, 0, 1)
+    value1[merge]()
+    key0[near]()
+    value0[row]()
+    work(weigh, 1, 1, 1)
+    key0[far]()
+    value1[row]()
     spread(1, 1)
-    spread(0, 1)
-    close2()
-    close3()
+    key0[close]()
     rows_arrived()
-
-    def ahead_step(i, carry):
-        attend(0, shift(place.z, 1 + 2 * i))
-        return carry
-
-    def rest_step(i, carry):
-        attend(0, shift(place.z, 2 + 2 * i))
-        return carry
-
-    value0, key0, value1, key1 = [
-        scatter_stage(kv, slot) for kv, slot in ((1, 0), (0, 0), (1, 1), (0, 1))
-    ]
-    start, relay, total, expand = range(4)
-    value1[start]()
-    key1[start]()
-    lax.fori_loop(0, 2, ahead_step, 0)
+    work(weigh, 0, 1, 2)
+    value0[near]()
+    value_grad1[start]()
+    work(weigh, 0, 2, 2)
+    value0[far]()
+    value1[near]()
+    spread(1, 0)
+    value0[close]()
+    value_grad1[relay]()
+    value_grad0[start]()
+    work(attend, 0, 1, 2)
     send_result(shift(place.z, 1), 1)
     send_result(shift(place.z, -1), -1)
-    value1[relay]()
-    key1[relay]()
-    lax.fori_loop(0, 2, rest_step, 0)
+    value1[far]()
+    value_grad0[relay]()
+    value_grad1[total]()
+    work(attend, 0, 2, 2)
     send_result(shift(place.z, 2), 2)
     send_result(place.z, 0)
-    value1[total]()
-    key1[total]()
-    spread(1, 0)
-    value0[start]()
-    value0[relay]()
-    value1[expand]()
-    key1[expand]()
+    value1[close]()
     spread(0, 0)
-    key0[start]()
-    key0[relay]()
-    value0[total]()
-    value0[expand]()
-    key0[total]()
-    key0[expand]()
+    value_grad1[expand]()
+    value_grad0[total]()
+    key_grad0[start]()
+    work(attend, 1, 0, 2)
+    send_pair_result()
+    spread(0, 1)
+    value_grad0[expand]()
+    key_grad0[relay]()
+    key_grad1[start]()
+    key_grad1[relay]()
+    key_grad0[total]()
+    key_grad0[expand]()
+    key_grad1[total]()
+    key_grad1[expand]()
 
     for which, (_, dst) in enumerate(results):
         for step in STEPS:
@@ -562,30 +602,6 @@
     links.finish()
 
 
-def prepare_kernel(pattern, live, spots, entries, biases):
-    place = Place()
-    for unit in range(sum(SLOT_UNITS)):
-        z = unit if unit < SIDE else place.z if unit == SIDE else place.partner_z()
-        frame = (place.y * SIDE + z) * CORES + place.core
-        base = unit % SIDE * ENTRIES
-
-        def clear(i, carry, unit=unit, base=base):
-            entries[unit * ALL_SPOTS + i] = base + DEAD
-            return carry
-
-        lax.fori_loop(0, ALL_SPOTS, clear, 0, unroll=8)
-
-        def note(j, carry, unit=unit, base=base, frame=frame):
-            spot = spot_of(pattern[j, frame])
-            alive = j < live[frame]
-            spots[unit * NSEL + j] = spot
-            biases[unit * NSEL + j] = jnp.where(alive, 0.0, -jnp.inf).astype(F32)
-            entries[unit * ALL_SPOTS + spot] = jnp.where(alive, base + j, base + DEAD)
-            return carry
-
-        lax.fori_loop(0, NSEL, note, 0, unroll=4)
-
-
 def store_kernel(*refs):
     sems = refs[-1]
     copies = [pltpu.make_async_copy(refs[i], refs[4 + i], sems.at[i]) for i in range(4)]
@@ -598,30 +614,19 @@
 ANY = pl.BlockSpec(memory_space=pl.ANY)
 HBM = pl.BlockSpec(memory_space=pltpu.HBM)
 VMEM = pl.BlockSpec(memory_space=pltpu.VMEM)
-SMEM = pl.BlockSpec(memory_space=pltpu.SMEM)
 
 
 def body(queries, keys_in, values_in, grad_out, assign, pattern, live_blocks):
     inputs = [
         pltpu.with_memory_space_constraint(one, pltpu.HBM)
-        for one in (keys_in, values_in, queries, grad_out, assign.reshape(1, TOK))
+        for one in (
+            keys_in, values_in, queries, grad_out, assign.reshape(1, TOK), pattern.T,
+            live_blocks.reshape(1, ALL_FRAMES),
+        )
     ]
     shape = jax.ShapeDtypeStruct
     dma = pltpu.SemaphoreType.DMA
     units = sum(SLOT_UNITS)
-    lists = pl.pallas_call(
-        prepare_kernel,
-        out_shape=(
-            shape((units * NSEL,), jnp.int32),
-            shape((units * ALL_SPOTS,), jnp.int32),
-            shape((units * NSEL,), F32),
-        ),
-        in_specs=[SMEM] * 2,
-        out_specs=(SMEM,) * 3,
-        compiler_params=pltpu.CompilerParams(vmem_limit_bytes=STORE_LIMIT),
-        name="prepare",
-    )(pattern.T, live_blocks)
-
     def half(*dims):
         return pltpu.VMEM(dims, BF)
 
@@ -633,7 +638,7 @@
             shape(keys_in.shape, BF),
             shape(keys_in.shape, BF),
         ),
-        in_specs=[HBM] * 5 + [SMEM] * 3,
+        in_specs=[HBM] * 7,
         out_specs=(ANY,) * 4,
         scratch_shapes=[
             half(ALL_SPOTS, KB, HD),
@@ -646,8 +651,8 @@
             half(units, TOK, HD),
             half(units, TOK, HD),
             half(NSEL * KB, HD),
-            half(NSEL * KB, HD),
-            pltpu.VMEM((NSEL * KB, TOK), F32),
+            pltpu.VMEM((units, NSEL * KB, TOK), F32),
+            pltpu.VMEM((units, 1, TOK), F32),
             pltpu.VMEM((NSEL * KB, TOK), F32),
             half(SLOT_UNITS[0] * ENTRIES, KB, HD),
             half(SLOT_UNITS[1] * ENTRIES, KB, HD),
@@ -663,6 +668,10 @@
             half(2, 2, GROUP, KB, HD),
             half(2, 2, SIDE, 2, KB, HD),
             half(2, TOK, WIDTH),
+            pltpu.SMEM((NSEL, ALL_FRAMES), jnp.int32),
+            pltpu.SMEM((1, ALL_FRAMES), jnp.int32),
+            pltpu.VMEM((8, HD), jnp.int32),
+            pltpu.SMEM((8, HD), jnp.int32),
             dma((SEMS,)),
             dma((SEMS,)),
             dma((LOCAL,)),
@@ -671,7 +680,7 @@
             collective_id=0, has_side_effects=True, vmem_limit_bytes=VMEM_LIMIT
         ),
         name="layer",
-    )(*inputs, *lists)
+    )(*inputs)
     return pl.pallas_call(
         store_kernel,
         out_shape=tuple(shape(one.shape, BF) for one in results),

time: 102 us -> 92.5 us (0.907)
  Pallas kernels: 100 us -> 91.6 us
  local copies, waits for them, and re-layouts: 1.34 us -> 0 us
    pallas_call x1, Pallas kernels: 94.4 us -> 89.9 us  [body(): pl.pallas_call(layer_kernel, out_shape=(shape(queries.shape, BF), shape(q...]
    pallas_call x1 -> x0, Pallas kernels: 3.92 us -> none  [body(): pl.pallas_call(prepare_kernel, out_shape=(shape((units * NSEL,), jnp.int3...]
    unnamed x4 -> x0, local copies, waits for them, and re-layouts: 1.34 us -> none
where the time goes in v6:
time: 92.5 us; the launch traced here: 92.4 us
  Pallas kernels  91.6 us (99%)
    pallas_call x1, Pallas kernels, body(): pl.pallas_call(layer_kernel, out_shape=(shape(queries.shape, BF), shape(q...  89.9 us

profile of v6, /device:TPU:0, one launch (start us, length us, event | category | flops | bytes accessed | tf_op | source)
XLA Modules:
  0.0 92.4 jit_solution(15226978835082651645)
XLA Ops:
  0.6 89.9 %layer.1 = (bf16[512,768]{1,0:T(8,128)(2,1)S(1)}, bf16[512,768]{1,0:T(8,128)(2,1)S(1)}, bf16[128,3072]{1,0:T(8,128)(2,1)S(1)}, bf16[128,3072]{1,0:T(8,128)(2,1)S(1)}) custom-call(bf16[128,3072]{1,0:T(8,128)(2,1)} %keys.1, bf16[128,3072]{1,0:T(8,128)(2,1)} %values.1, bf16[512,768]{1,0:T(8,128)(2,1)} %queries.1, bf16[512,768]{1,0:T(8,128)(2,1)} %upstream.1, ...), custom_call_target="tpu_custom_call" | custom-call | tf_op jit(solution)/shard_map/layer/pallas_call | solution.py:633
  90.5 1.7 %store.1 = (bf16[512,768]{1,0:T(8,128)(2,1)}, bf16[512,768]{1,0:T(8,128)(2,1)}, bf16[128,3072]{1,0:T(8,128)(2,1)}, bf16[128,3072]{1,0:T(8,128)(2,1)}) custom-call(bf16[512,768]{1,0:T(8,128)(2,1)S(1)} %get-tuple-element.8.refs_0_, bf16[512,768]{1,0:T(8,128)(2,1)S(1)} %get-tuple-element.9.refs_1_, bf16[128,3072]{1,0:T(8,128)(2,1)S(1)} %get-tuple-element.10.refs_2_, ...), custom_call_target="tpu_custom_call" | custom-call | tf_op jit(solution)/shard_map/store/pallas_call | solution.py:684

commit v7 on v6

--- a/solution.py
+++ b/solution.py
@@ -30,8 +30,8 @@
 STEPS = (1, -1, 2)
 GROUPS = ((0, SIDE), (SIDE, HEADS_X - SIDE))
 GATHER_PARTS = ((0, 1), (0, 0), (1, 0), (1, 1))
-GATHER_STRAIGHT = (GATHER_PARTS[0], GATHER_PARTS[3])
-SCATTER_STRAIGHT = ()
+GATHER_STRAIGHT = (GATHER_PARTS[0],)
+SCATTER_STRAIGHT = ((0, 0),)
 
 
 class Place:
@@ -573,11 +573,11 @@
     value_grad1[expand]()
     value_grad0[total]()
     key_grad0[start]()
+    key_grad0[relay]()
     work(attend, 1, 0, 2)
     send_pair_result()
     spread(0, 1)
     value_grad0[expand]()
-    key_grad0[relay]()
     key_grad1[start]()
     key_grad1[relay]()
     key_grad0[total]()

time: 92.5 us -> 85.5 us (0.924); the launches traced: 92.4 us -> 84.4 us
  Pallas kernels: 91.6 us -> 83.6 us
    pallas_call x1, Pallas kernels: 89.9 us -> 81.9 us  [body(): pl.pallas_call(layer_kernel, out_shape=(shape(queries.shape, BF), shape(q...]
where the time goes in v7:
time: 85.5 us; the launch traced here: 84.4 us
  Pallas kernels  83.6 us (98%)
    pallas_call x1, Pallas kernels, body(): pl.pallas_call(layer_kernel, out_shape=(shape(queries.shape, BF), shape(q...  81.9 us

profile of v7, /device:TPU:0, one launch (start us, length us, event | category | flops | bytes accessed | tf_op | source)
XLA Modules:
  0.0 84.4 jit_solution(11658495851969929111)
XLA Ops:
  0.6 81.9 %layer.1 = (bf16[512,768]{1,0:T(8,128)(2,1)S(1)}, bf16[512,768]{1,0:T(8,128)(2,1)S(1)}, bf16[128,3072]{1,0:T(8,128)(2,1)S(1)}, bf16[128,3072]{1,0:T(8,128)(2,1)S(1)}) custom-call(bf16[128,3072]{1,0:T(8,128)(2,1)} %keys.1, bf16[128,3072]{1,0:T(8,128)(2,1)} %values.1, bf16[512,768]{1,0:T(8,128)(2,1)} %queries.1, bf16[512,768]{1,0:T(8,128)(2,1)} %upstream.1, ...), custom_call_target="tpu_custom_call" | custom-call | tf_op jit(solution)/shard_map/layer/pallas_call | solution.py:633
  82.6 1.7 %store.1 = (bf16[512,768]{1,0:T(8,128)(2,1)}, bf16[512,768]{1,0:T(8,128)(2,1)}, bf16[128,3072]{1,0:T(8,128)(2,1)}, bf16[128,3072]{1,0:T(8,128)(2,1)}) custom-call(bf16[512,768]{1,0:T(8,128)(2,1)S(1)} %get-tuple-element.8.refs_0_, bf16[512,768]{1,0:T(8,128)(2,1)S(1)} %get-tuple-element.9.refs_1_, bf16[128,3072]{1,0:T(8,128)(2,1)S(1)} %get-tuple-element.10.refs_2_, ...), custom_call_target="tpu_custom_call" | custom-call | tf_op jit(solution)/shard_map/store/pallas_call | solution.py:684

commit v8 on v7

--- a/solution.py
+++ b/solution.py
@@ -422,7 +422,7 @@
                 dense[kv, slot, spot] = total.astype(BF)
                 return carry
 
-            lax.fori_loop(0, GROUP, one, 0)
+            lax.fori_loop(0, GROUP, one, 0, unroll=GROUP)
 
         for step in (2, 1, -1, 0):
             y = shift(place.y, step)
@@ -579,8 +579,8 @@
     spread(0, 1)
     value_grad0[expand]()
     key_grad1[start]()
+    key_grad0[total]()
     key_grad1[relay]()
-    key_grad0[total]()
     key_grad0[expand]()
     key_grad1[total]()
     key_grad1[expand]()

time: 85.5 us -> 84.6 us (0.989)
  Pallas kernels: 83.6 us -> 82.6 us
    pallas_call x1, Pallas kernels: 81.9 us -> 80.9 us  [body(): pl.pallas_call(layer_kernel, out_shape=(shape(queries.shape, BF), shape(q...]
where the time goes in v8:
time: 84.6 us; the launch traced here: 83.4 us
  Pallas kernels  82.6 us (98%)
    pallas_call x1, Pallas kernels, body(): pl.pallas_call(layer_kernel, out_shape=(shape(queries.shape, BF), shape(q...  80.9 us
    pallas_call x1, Pallas kernels, body(): pl.pallas_call(store_kernel, out_shape=tuple((shape(one.shape, BF) for on...  1.69 us

profile of v8, /device:TPU:0, one launch (start us, length us, event | category | flops | bytes accessed | tf_op | source)
XLA Modules:
  0.0 83.4 jit_solution(9148796863666141742)
XLA Ops:
  0.6 80.9 %layer.1 = (bf16[512,768]{1,0:T(8,128)(2,1)S(1)}, bf16[512,768]{1,0:T(8,128)(2,1)S(1)}, bf16[128,3072]{1,0:T(8,128)(2,1)S(1)}, bf16[128,3072]{1,0:T(8,128)(2,1)S(1)}) custom-call(bf16[128,3072]{1,0:T(8,128)(2,1)} %keys.1, bf16[128,3072]{1,0:T(8,128)(2,1)} %values.1, bf16[512,768]{1,0:T(8,128)(2,1)} %queries.1, bf16[512,768]{1,0:T(8,128)(2,1)} %upstream.1, ...), custom_call_target="tpu_custom_call" | custom-call | tf_op jit(solution)/shard_map/layer/pallas_call | solution.py:633
  81.6 1.7 %store.1 = (bf16[512,768]{1,0:T(8,128)(2,1)}, bf16[512,768]{1,0:T(8,128)(2,1)}, bf16[128,3072]{1,0:T(8,128)(2,1)}, bf16[128,3072]{1,0:T(8,128)(2,1)}) custom-call(bf16[512,768]{1,0:T(8,128)(2,1)S(1)} %get-tuple-element.8.refs_0_, bf16[512,768]{1,0:T(8,128)(2,1)S(1)} %get-tuple-element.9.refs_1_, bf16[128,3072]{1,0:T(8,128)(2,1)S(1)} %get-tuple-element.10.refs_2_, ...), custom_call_target="tpu_custom_call" | custom-call | tf_op jit(solution)/shard_map/store/pallas_call | solution.py:684
